TPU v7x, 512 devices: a whole 4x4x16 slice. The times are simulated.
512 devices in a mesh: tm: 8 (over y, z_hi), space: 64 (over x, z_lo, core).
Axes of the slice: x: 4, y: 4, z: 16 (z_hi: 2, z_lo: 8; z = z_hi * 8 + z_lo), core: 2. Of those that a mesh axis runs over, the one named last changes fastest.
Arguments:
- start_state: float32 [8, 3, 512, 2048], P('tm', None, 'space'), may hold values from -4 to 4
- vertical_field: float32 [512, 2048], P('space'), may hold values from -1 to 1
Outputs:
- new_start: float32 [8, 3, 512, 2048], P('tm', None, 'space')
- fine_end: float32 [8, 3, 512, 2048], P('tm', None, 'space')
- coarse_end: float32 [8, 3, 512, 2048], P('tm', None, 'space')
All inputs are finite; a program needn't handle non-finite values.
Results may differ from a plain program's by a relative error of at most 0.0001.
Values sent between devices are 32-bit elements; how exact they have to be, the bound alone decides.
No kernel may reach another device: no remote copies, remote signals or barrier semaphores. Data moves between devices by JAX's collectives and lax.ppermute only.
A program may use at most 64 MiB of HBM per device.

v0:
```python
import functools

import jax
import jax.numpy as jnp
from jax import lax
from jax.experimental import pallas as pl
from jax.experimental.pallas import tpu as pltpu
from jax.sharding import PartitionSpec as P

FINE_STEPS = 8
LORENTZ = 0.3
FRICTION = 0.01
TIME_STEP = 0.28
ROWS = 8
LANES = 128
GROUP = 8

ALPHA = 0.6265382932707997
QUAD_A = 0.3734617067292003
QUAD_B = 0.2660119396638869

VMEM = pl.BlockSpec(memory_space=pltpu.VMEM)
SMEM = pl.BlockSpec(memory_space=pltpu.SMEM)


def iotas():
    sub = lax.broadcasted_iota(jnp.int32, (ROWS, LANES), 0)
    lane = lax.broadcasted_iota(jnp.int32, (ROWS, LANES), 1)
    return sub, lane


def strip(k):
    start = LANES + k * LANES
    return pl.ds(start if isinstance(start, int) else pl.multiple_of(start, LANES), LANES)


def guards(buf, tiles, shift, strips):
    _, lane = iotas()
    even = lane % 2 == 0
    for t in tiles:
        for comp, sign in ((0, 1.0), (2, -1.0)):
            first = buf[t, comp, :, strip(0)]
            last = buf[t, comp, :, strip(strips - 1)]
            low = sign * pltpu.roll(first, LANES - shift, 1)
            high = sign * pltpu.roll(last, shift, 1)
            if shift == 2:
                low = jnp.where(even, low, pltpu.roll(last, 1, 1))
                high = jnp.where(even, pltpu.roll(first, LANES - 1, 1), high)
            buf[t, comp, :, strip(-1)] = low
            buf[t, comp, :, strip(strips)] = high


def stage(dst, src, base, weight, length, field, tiles, shift, cell, strips, group):
    factor = length / (2.0 * cell)
    drag = FRICTION * length
    sub, lane = iotas()
    rows_high = sub >= ROWS - shift
    rows_low = sub < shift
    lanes_high = lane >= LANES - shift
    lanes_low = lane < shift
    slots = dst.shape[0]
    group = min(group, strips)

    def block(g, carry):
        for j in range(group):
            k = g * group + j
            here = strip(k)
            cache = {}

            def get(comp, t):
                t = min(max(t, 0), slots - 1)
                if (comp, t) not in cache:
                    cache[comp, t] = src[t, comp, :, here]
                return cache[comp, t]

            for t in tiles:
                height, east, north = get(0, t), get(1, t), get(2, t)

                def row_diff(comp, centre):
                    before = jnp.where(rows_high, get(comp, t - 1), centre)
                    after = jnp.where(rows_low, get(comp, t + 1), centre)
                    return pltpu.roll(after, ROWS - shift, 0) - pltpu.roll(before, shift, 0)

                def col_diff(comp, centre):
                    before = jnp.where(lanes_high, src[t, comp, :, strip(k - 1)], centre)
                    after = jnp.where(lanes_low, src[t, comp, :, strip(k + 1)], centre)
                    return pltpu.roll(after, LANES - shift, 1) - pltpu.roll(before, shift, 1)

                b = field[t, :, pl.ds(here.start - LANES, LANES)]
                dx, dy = row_diff(0, height), col_diff(0, height)
                rise = row_diff(1, east) + col_diff(2, north)
                if base is src:
                    new_height = weight * height - factor * rise
                    new_east = (weight - drag) * east + factor * (b * dy - dx)
                    new_north = (weight - drag) * north - factor * (b * dx + dy)
                else:
                    old = [base[t, comp, :, here] for comp in range(3)]
                    if weight != 1.0:
                        old = [weight * o for o in old]
                    new_height = old[0] - factor * rise
                    new_east = old[1] - drag * east + factor * (b * dy - dx)
                    new_north = old[2] - drag * north - factor * (b * dx + dy)
                dst[t, 0, :, here] = new_height
                dst[t, 1, :, here] = new_east
                dst[t, 2, :, here] = new_north
        return carry

    lax.fori_loop(0, strips // group, block, 0)
    guards(dst, tiles, shift, strips)


def pair_mean(x, sub, lane):
    x = x + jnp.where(sub % 2 == 0, pltpu.roll(x, ROWS - 1, 0), pltpu.roll(x, 1, 0))
    x = x + jnp.where(lane % 2 == 0, pltpu.roll(x, LANES - 1, 1), pltpu.roll(x, 1, 1))
    return 0.25 * x


def flip_tiles(position, count, halo, first, copy_row):
    low = jnp.maximum(halo - position, 0)
    high = jnp.maximum(position + halo - (count - 1), 0)

    def fill_low(q, carry):
        for r in range(ROWS):
            copy_row(first + halo - position - 1 - q, ROWS - 1 - r, first + halo - position + q, r)
        return carry

    def fill_high(q, carry):
        for r in range(ROWS):
            copy_row(
                first + count + q - position + halo,
                ROWS - 1 - r,
                first + count - 1 - q - position + halo,
                r,
            )
        return carry

    lax.fori_loop(0, low, fill_low, 0)
    lax.fori_loop(0, high, fill_high, 0)


def flip_state(buf, position, count, halo, first=0):
    cols = pl.ds(LANES, buf.shape[3] - 2 * LANES)

    def copy_row(t_to, r_to, t_from, r_from):
        for comp, sign in ((0, 1.0), (1, -1.0), (2, 1.0)):
            buf[t_to, comp, pl.ds(r_to, 1), cols] = sign * buf[t_from, comp, pl.ds(r_from, 1), cols]

    flip_tiles(position, count, halo, first, copy_row)


def flip_field(field, position, count, halo):
    def copy_row(t_to, r_to, t_from, r_from):
        field[t_to, pl.ds(r_to, 1), :] = -field[t_from, pl.ds(r_from, 1), :]

    flip_tiles(position, count, halo, 0, copy_row)


def folded(left, right, lane):
    return jnp.where(lane % 2 == 0, left, right)


def unfolded(x, lane):
    left = jnp.where(lane % 2 == 0, x, pltpu.roll(x, 1, 1))
    right = jnp.where(lane % 2 == 1, x, pltpu.roll(x, LANES - 1, 1))
    return left, right


def zipped(even, odd, sub):
    return jnp.where(sub % 2 == 0, even, odd)


def unzipped(x, sub):
    even = jnp.where(sub % 2 == 0, x, pltpu.roll(x, 1, 0))
    odd = jnp.where(sub % 2 == 1, x, pltpu.roll(x, ROWS - 1, 0))
    return even, odd


def places(position):
    core = lax.rem(position, 2)
    chip = lax.div(position, 2)
    side = 1 - 2 * core
    near = 2 * (2 * lax.rem(chip, 2) - 1)
    far = 4 * (2 * lax.rem(lax.div(chip, 2), 2) - 1)
    return side, near, far


def fine_kernel(
    count, strips, pos, state, field, near_a, near_b, third, sib, sib_a, sib_b, coarse,
    out, detail, message, one, two, window,
):
    position = pos[0]
    side, near, _ = places(position)
    cols = pl.ds(LANES, strips * LANES)
    arrived = (
        (near_a, near), (near_b, -near), (third, -3 * side),
        (sib, side), (sib_a, near + side), (sib_b, side - near),
    )
    window[3] = LORENTZ * field[...]
    for comp in range(3):
        one[3, comp, :, cols] = state[comp]
    for ref, offset in arrived:
        slot = 3 + offset
        window[slot] = LORENTZ * ref[3]
        for comp in range(3):
            one[slot, comp, :, cols] = ref[comp]
    flip_field(window, position, count, 3)
    flip_state(one, position, count, 3)
    guards(one, range(7), 1, strips)

    run = functools.partial(stage, field=window, shift=1, cell=1.0, strips=strips, group=GROUP)
    a, b = one, two
    for reach, quads, lines in ((3, 3, 2), (2, 3, 2), (1, 2, 4)):
        tiles = range(3 - reach, 4 + reach)

        def quad(step, carry, a=a, b=b, tiles=tiles):
            run(b, a, a, QUAD_A, QUAD_B * TIME_STEP, tiles=tiles)
            run(a, b, a, 1.0, TIME_STEP, tiles=tiles)
            return carry

        lax.fori_loop(0, quads, quad, 0)
        for n in range(lines):
            if n == lines - 1:
                tiles = range(4 - reach, 3 + reach)
            run(b, a, a, 1.0, ALPHA * TIME_STEP, tiles=tiles)
            a, b = b, a

    sub, lane = iotas()
    keep = jnp.where(pos[1] == 0, 0.0, 1.0)
    half = strips // 2
    for k in range(half):
        means = []
        for comp in range(3):
            sides = []
            for s in (k, k + half):
                lanes = pl.ds(s * LANES, LANES)
                value = a[3, comp, :, strip(s)]
                out[comp, :, lanes] = value
                rest = value - keep * coarse[comp, :, lanes]
                detail[comp, :, lanes] = rest
                sides.append(pair_mean(rest, sub, lane))
            means.append(folded(*sides, lane))
        sides = [pair_mean(field[:, pl.ds(s * LANES, LANES)], sub, lane) for s in (k, k + half)]
        lanes = pl.ds(k * LANES, LANES)
        message[0, :, lanes] = zipped(means[0], means[1], sub)
        message[1, :, lanes] = zipped(means[2], LORENTZ * folded(*sides, lane), sub)


def coarse_step(bufs, field, tiles_of, strips, group):
    one, two, three = bufs
    length = FINE_STEPS * TIME_STEP
    run = functools.partial(stage, base=one, field=field, shift=2, cell=2.0, strips=strips, group=group)
    run(two, one, weight=1.0, length=length / 3.0, tiles=tiles_of(0))
    run(three, two, weight=1.0, length=length / 2.0, tiles=tiles_of(1))
    run(one, three, weight=1.0, length=length, tiles=tiles_of(2))


def coarse_kernel(count, strips, pos, state, field, sib, sib_a, sib_b, out, one, two, three, window):
    position = pos[0]
    side, near, _ = places(position)
    sub, lane = iotas()
    half = strips // 2

    def put(slot, ref, plane):
        for k in range(half):
            pairs = [pl.ds(s * LANES, LANES) for s in (k, k + half)]
            for comp in range(3):
                means = [pair_mean(ref[comp, :, lanes], sub, lane) for lanes in pairs]
                one[slot, comp, :, strip(k)] = folded(*means, lane)
            means = [pair_mean(plane[:, lanes], sub, lane) for lanes in pairs]
            window[slot, :, pl.ds(k * LANES, LANES)] = LORENTZ * folded(*means, lane)

    put(1, state, field)
    put(1 + side, sib, sib.at[3])
    for ref, sign in ((sib_a, 1), (sib_b, -1)):

        @pl.when(sign * near + side == -side)
        def _(ref=ref):
            put(1 - side, ref, ref.at[3])

    flip_field(window, position, count, 1)
    flip_state(one, position, count, 1)
    guards(one, range(3), 2, half)
    coarse_step((one, two, three), window, lambda n: range(3) if n < 2 else (1,), half, GROUP)
    for k in range(half):
        for comp in range(3):
            for s, value in zip((k, k + half), unfolded(one[1, comp, :, strip(k)], lane)):
                out[comp, :, pl.ds(s * LANES, LANES)] = value


def powers_kernel(
    count, strips, pos, own, sib, near_a, sib_a, near_b, sib_b, far_a, far_sa, far_b, far_sb, fifth,
    *refs,
):
    outs, (one, two, three, window) = refs[:3], refs[3:]
    position = pos[0]
    side, near, far = places(position)
    sub, lane = iotas()
    half = strips // 2
    arrived = (
        (own, 0), (sib, side), (near_a, near), (sib_a, near + side), (near_b, -near),
        (sib_b, side - near), (far_a, far), (far_sa, far + side), (far_b, -far),
        (far_sb, side - far), (fifth, -5 * side),
    )
    for ref, offset in arrived:
        slot = 5 + offset
        for k in range(half):
            lanes = pl.ds(k * LANES, LANES)
            height, east = unzipped(ref[0, :, lanes], sub)
            north, plane = unzipped(ref[1, :, lanes], sub)
            one[slot, 0, :, strip(k)] = height
            one[slot, 1, :, strip(k)] = east
            one[slot, 2, :, strip(k)] = north
            window[slot, :, lanes] = plane
    flip_field(window, position, count, 5)
    flip_state(one, position, count, 5)
    guards(one, range(11), 2, half)
    for s in range(6):

        def tiles_of(n, s=s):
            reach = -(-2 * (18 - 3 * s - n - 1) // ROWS)
            return range(5 - reach, 6 + reach)

        coarse_step((one, two, three), window, tiles_of, half, 4)
        out = outs[s // 2]
        for k in range(half):
            lanes = pl.ds(k * LANES, LANES)
            height, east, north = [one[5, comp, :, strip(k)] for comp in range(3)]
            out[s % 2, :, lanes] = zipped(height, east, sub)
            if s % 2 == 0:
                out[2, :, lanes] = north
            else:
                out[2, :, lanes] = zipped(out[2, :, lanes], north, sub)


def final_kernel(strips, pos, own, other, detail, anchor, out):
    sub, lane = iotas()
    half = strips // 2
    first = pos[1] == 0
    for k in range(half):
        lanes = pl.ds(k * LANES, LANES)
        height, east = unzipped(own[0, :, lanes] + other[1, :, lanes], sub)
        north = unzipped(own[2, :, lanes], sub)[0] + unzipped(other[2, :, lanes], sub)[1]
        for comp, value in enumerate((height, east, north)):
            for s, part in zip((k, k + half), unfolded(value, lane)):
                wide = pl.ds(s * LANES, LANES)
                total = part + detail[comp, :, wide]
                out[comp, :, wide] = jnp.where(first, anchor[comp, :, wide], total)


def call(kernel, outs, buffers, name, *args):
    return pl.pallas_call(
        kernel,
        out_shape=outs,
        in_specs=[SMEM] + [VMEM] * (len(args) - 1),
        out_specs=[VMEM] * len(outs),
        scratch_shapes=buffers,
        compiler_params=pltpu.CompilerParams(vmem_limit_bytes=48 * 1024 * 1024),
        name=name,
    )(*args)


def swap(block, partner):
    slices, count = lax.axis_size("tm"), lax.axis_size("space")
    pairs = [(i, partner(i)) for i in range(count)]
    pairs = [(i, j) for i, j in pairs if 0 <= j < count]
    return lax.ppermute(block, "space", pairs)


def later(block, distance):
    slices = lax.axis_size("tm")
    return lax.ppermute(block, "tm", [(m, m + distance) for m in range(slices - distance)])


def sibling(i):
    return i + 1 - 2 * (i % 2)


def near_odd(i):
    return i + (2 if (i // 2) % 2 == 1 else -2)


def near_even(i):
    return i - (2 if (i // 2) % 2 == 1 else -2)


def far_odd(i):
    return i + (4 if (i // 4) % 2 == 1 else -4)


def far_even(i):
    return i - (4 if (i // 4) % 2 == 1 else -4)


def third(i):
    return i - 3 if i % 2 == 0 else i + 3


def fifth(i):
    return i - 5 if i % 2 == 0 else i + 5


def body(start_state, vertical_field):
    state = start_state[0]
    cols = state.shape[2]
    strips = cols // LANES
    count = lax.axis_size("space")
    pos = jnp.stack([lax.axis_index("space"), lax.axis_index("tm")]).astype(jnp.int32)
    shape = lambda *dims: jax.ShapeDtypeStruct(dims, jnp.float32)
    tile = shape(3, ROWS, cols)
    buf = lambda tiles, wide: pltpu.VMEM((tiles, 3, ROWS, wide + 2 * LANES), jnp.float32)
    plane = lambda tiles, wide: pltpu.VMEM((tiles, ROWS, wide), jnp.float32)

    sent = jnp.concatenate([state, vertical_field[None]], axis=0)
    sib = swap(sent, sibling)
    b = swap(sent, near_even)
    q = swap(sent, third)
    a = swap(sent, near_odd)
    sib_b, sib_a = swap(b, sibling), swap(a, sibling)
    (coarse_end,) = call(
        functools.partial(coarse_kernel, count, strips),
        [tile],
        [buf(3, cols // 2)] * 3 + [plane(3, cols // 2)],
        "coarse",
        pos, state, vertical_field, sib, sib_a, sib_b,
    )
    fine_end, detail, message = call(
        functools.partial(fine_kernel, count, strips),
        [tile, tile, shape(2, ROWS, cols // 2)],
        [buf(7, cols), buf(7, cols), plane(7, cols)],
        "fine",
        pos, state, vertical_field, a, b, q, sib, sib_a, sib_b, coarse_end,
    )
    arrived = later(detail, 1)
    sib = swap(message, sibling)
    b = swap(message, near_even)
    d = swap(message, far_even)
    q = swap(message, fifth)
    c = swap(message, far_odd)
    a = swap(message, near_odd)
    sib_b, sib_d, sib_c, sib_a = [swap(x, sibling) for x in (b, d, c, a)]
    powers = call(
        functools.partial(powers_kernel, count, strips),
        [shape(3, ROWS, cols // 2)] * 3,
        [buf(11, cols // 2)] * 3 + [plane(11, cols // 2)],
        "powers",
        pos, message, sib, a, sib_a, b, sib_b, c, sib_c, d, sib_d, q,
    )
    own = sum(later(x, 2 * d + 2) for d, x in enumerate(powers))
    other = later(own, 1)
    (new_start,) = call(
        functools.partial(final_kernel, strips),
        [tile],
        [],
        "final",
        pos, own, other, arrived, state,
    )
    return (new_start[None], fine_end[None], coarse_end[None])


def solution(mesh):
    in_specs = (P("tm", None, "space", None), P("space", None))
    out_specs = (
        P("tm", None, "space", None),
        P("tm", None, "space", None),
        P("tm", None, "space", None),
    )
    return jax.shard_map(body, mesh=mesh, in_specs=in_specs, out_specs=out_specs, check_vma=False)
```

profile of v0, /device:TPU:10, one launch (start us, length us, event | category | flops | bytes accessed | tf_op | source)
XLA Modules:
  0.0 156.8 jit_solution(7487941924629140131)
XLA Ops:
  1.7 3.8 %collective-permute-start.1 = (f32[4,8,2048]{2,1,0:T(8,128)S(1)}, f32[4,8,2048]{2,1,0:T(8,128)S(1)}, u32[]{:S(2)}, u32[]{:S(2)}) collective-permute-start(f32[4,8,2048]{2,1,0:T(8,128)S(1)} %pad_maximum_fusion), channel_id=1, source_target_pairs={{0,2},{1,3},{2,0},{3,1},{4,6},{5,7},{6,4},{7,5},{8,10},{9,11},{10,... | collective-permute-start | bytes 786440 | tf_op jit(solution)/shard_map/ppermute | solution.py:366
  5.5 11.3 %collective-permute-start = (f32[4,8,2048]{2,1,0:T(8,128)S(1)}, f32[4,8,2048]{2,1,0:T(8,128)S(1)}, u32[]{:S(2)}, u32[]{:S(2)}) collective-permute-start(f32[4,8,2048]{2,1,0:T(8,128)S(1)} %pad_maximum_fusion), channel_id=1, source_target_pairs={{2,4},{3,5},{4,2},{5,3},{6,8},{7,9},{8,6},{9,7},{10,12},{11,13},{1... | collective-permute-start | bytes 786440 | tf_op jit(solution)/shard_map/ppermute | solution.py:366
  16.8 1.9 %collective-permute-start.3 = (f32[4,8,2048]{2,1,0:T(8,128)S(1)}, f32[4,8,2048]{2,1,0:T(8,128)S(1)}, u32[]{:S(2)}, u32[]{:S(2)}) collective-permute-start(f32[4,8,2048]{2,1,0:T(8,128)S(1)} %pad_maximum_fusion), channel_id=1, source_target_pairs={{0,1},{1,0},{2,3},{3,2},{4,5},{5,4},{6,7},{7,6},{8,9},{9,8},{10,11... | collective-permute-start | bytes 786440 | tf_op jit(solution)/shard_map/ppermute | solution.py:366
  18.8 2.4 %collective-permute-start.5 = (f32[4,8,2048]{2,1,0:T(8,128)S(1)}, f32[4,8,2048]{2,1,0:T(8,128)S(1)}, u32[]{:S(2)}, u32[]{:S(2)}) collective-permute-start(f32[4,8,2048]{2,1,0:T(8,128)S(1)} %collective-permute-done.1.near_b), channel_id=1, source_target_pairs={{0,1},{1,0},{2,3},{3,2},{4,5},{5,4},{6,7},{7,6},{8,9},{9,8},{10,11... | collective-permute-start | bytes 786440 | tf_op jit(solution)/shard_map/ppermute | solution.py:366
  21.2 5.7 %collective-permute-done.near_a = f32[4,8,2048]{2,1,0:T(8,128)S(1)} collective-permute-done((f32[4,8,2048]{2,1,0:T(8,128)S(1)}, f32[4,8,2048]{2,1,0:T(8,128)S(1)}, u32[]{:S(2)}, u32[]{:S(2)}) %collective-permute-start) | collective-permute-done | bytes 262176 | tf_op jit(solution)/shard_map/ppermute | solution.py:366
  28.8 3.6 %collective-permute-start.2 = (f32[4,8,2048]{2,1,0:T(8,128)S(1)}, f32[4,8,2048]{2,1,0:T(8,128)S(1)}, u32[]{:S(2)}, u32[]{:S(2)}) collective-permute-start(f32[4,8,2048]{2,1,0:T(8,128)S(1)} %pad_maximum_fusion), channel_id=1, source_target_pairs={{1,4},{3,6},{4,1},{5,8},{6,3},{7,10},{8,5},{9,12},{10,7},{11,14},{... | collective-permute-start | bytes 786440 | tf_op jit(solution)/shard_map/ppermute | solution.py:366
  32.5 2.4 %coarse.1 = f32[3,8,2048]{2,1,0:T(8,128)} custom-call(s32[2]{0:T(128)S(1)} %pad_add_fusion.pos, f32[3,8,2048]{2,1,0:T(8,128)S(1)} %bitcast.8, f32[8,2048]{1,0:T(8,128)S(1)} %copy-done.2, f32[4,8,2048]{2,1,0:T(8,128)S(1)} %collective-permute-done.3.sib, f32[4,8,2048]{2,1,0:T(8,128)S(1)} %collective-permute-done.4.sib_a, ...), custom_call_target="tpu_custom_call" | custom-call | tf_op jit(solution)/shard_map/coarse/pallas_call | solution.py:351
  34.9 11.1 %collective-permute-done.2.third = f32[4,8,2048]{2,1,0:T(8,128)S(1)} collective-permute-done((f32[4,8,2048]{2,1,0:T(8,128)S(1)}, f32[4,8,2048]{2,1,0:T(8,128)S(1)}, u32[]{:S(2)}, u32[]{:S(2)}) %collective-permute-start.2) | collective-permute-done | bytes 262176 | tf_op jit(solution)/shard_map/ppermute | solution.py:366
  46.9 15.2 %fine.1 = (f32[3,8,2048]{2,1,0:T(8,128)}, f32[3,8,2048]{2,1,0:T(8,128)S(1)}, f32[2,8,1024]{2,1,0:T(8,128)S(1)}) custom-call(s32[2]{0:T(128)S(1)} %pad_add_fusion.pos, f32[3,8,2048]{2,1,0:T(8,128)S(1)} %bitcast.9, f32[8,2048]{1,0:T(8,128)S(1)} %copy-done.2, f32[4,8,2048]{2,1,0:T(8,128)S(1)} %collective-permute-done.near_a, ...), custom_call_target="tpu_custom_call" | custom-call | tf_op jit(solution)/shard_map/fine/pallas_call | solution.py:351
  64.1 6.7 %collective-permute-start.13 = (f32[2,8,1024]{2,1,0:T(8,128)S(1)}, f32[2,8,1024]{2,1,0:T(8,128)S(1)}, u32[]{:S(2)}, u32[]{:S(2)}) collective-permute-start(f32[2,8,1024]{2,1,0:T(8,128)S(1)} %get-tuple-element.9.own), channel_id=1, source_target_pairs={{0,4},{1,5},{2,6},{3,7},{4,0},{5,1},{6,2},{7,3},{8,12},{9,13},{10,... | collective-permute-start | bytes 196616 | tf_op jit(solution)/shard_map/ppermute | solution.py:366
  70.8 1.9 %collective-permute-start.11 = (f32[2,8,1024]{2,1,0:T(8,128)S(1)}, f32[2,8,1024]{2,1,0:T(8,128)S(1)}, u32[]{:S(2)}, u32[]{:S(2)}) collective-permute-start(f32[2,8,1024]{2,1,0:T(8,128)S(1)} %get-tuple-element.9.own), channel_id=1, source_target_pairs={{4,8},{5,9},{6,10},{7,11},{8,4},{9,5},{10,6},{11,7},{12,16},{13,17... | collective-permute-start | bytes 196616 | tf_op jit(solution)/shard_map/ppermute | solution.py:366
  72.7 1.9 %collective-permute-start.9 = (f32[2,8,1024]{2,1,0:T(8,128)S(1)}, f32[2,8,1024]{2,1,0:T(8,128)S(1)}, u32[]{:S(2)}, u32[]{:S(2)}) collective-permute-start(f32[2,8,1024]{2,1,0:T(8,128)S(1)} %get-tuple-element.9.own), channel_id=1, source_target_pairs={{0,2},{1,3},{2,0},{3,1},{4,6},{5,7},{6,4},{7,5},{8,10},{9,11},{10,... | collective-permute-start | bytes 196616 | tf_op jit(solution)/shard_map/ppermute | solution.py:366
  74.6 12.0 %collective-permute-start.7 = (f32[2,8,1024]{2,1,0:T(8,128)S(1)}, f32[2,8,1024]{2,1,0:T(8,128)S(1)}, u32[]{:S(2)}, u32[]{:S(2)}) collective-permute-start(f32[2,8,1024]{2,1,0:T(8,128)S(1)} %get-tuple-element.9.own), channel_id=1, source_target_pairs={{2,4},{3,5},{4,2},{5,3},{6,8},{7,9},{8,6},{9,7},{10,12},{11,13},{1... | collective-permute-start | bytes 196616 | tf_op jit(solution)/shard_map/ppermute | solution.py:366
  86.6 1.9 %collective-permute-start.6 = (f32[2,8,1024]{2,1,0:T(8,128)S(1)}, f32[2,8,1024]{2,1,0:T(8,128)S(1)}, u32[]{:S(2)}, u32[]{:S(2)}) collective-permute-start(f32[2,8,1024]{2,1,0:T(8,128)S(1)} %get-tuple-element.9.own), channel_id=1, source_target_pairs={{0,1},{1,0},{2,3},{3,2},{4,5},{5,4},{6,7},{7,6},{8,9},{9,8},{10,11... | collective-permute-start | bytes 196616 | tf_op jit(solution)/shard_map/ppermute | solution.py:366
  88.5 2.4 %collective-permute-start.14 = (f32[2,8,1024]{2,1,0:T(8,128)S(1)}, f32[2,8,1024]{2,1,0:T(8,128)S(1)}, u32[]{:S(2)}, u32[]{:S(2)}) collective-permute-start(f32[2,8,1024]{2,1,0:T(8,128)S(1)} %collective-permute-done.13.far_b), channel_id=1, source_target_pairs={{0,1},{1,0},{2,3},{3,2},{4,5},{5,4},{6,7},{7,6},{8,9},{9,8},{10,11... | collective-permute-start | bytes 196616 | tf_op jit(solution)/shard_map/ppermute | solution.py:366
  91.0 1.9 %collective-permute-start.12 = (f32[2,8,1024]{2,1,0:T(8,128)S(1)}, f32[2,8,1024]{2,1,0:T(8,128)S(1)}, u32[]{:S(2)}, u32[]{:S(2)}) collective-permute-start(f32[2,8,1024]{2,1,0:T(8,128)S(1)} %collective-permute-done.11.far_a), channel_id=1, source_target_pairs={{0,1},{1,0},{2,3},{3,2},{4,5},{5,4},{6,7},{7,6},{8,9},{9,8},{10,11... | collective-permute-start | bytes 196616 | tf_op jit(solution)/shard_map/ppermute | solution.py:366
  92.9 2.4 %collective-permute-start.10 = (f32[2,8,1024]{2,1,0:T(8,128)S(1)}, f32[2,8,1024]{2,1,0:T(8,128)S(1)}, u32[]{:S(2)}, u32[]{:S(2)}) collective-permute-start(f32[2,8,1024]{2,1,0:T(8,128)S(1)} %collective-permute-done.9.near_b), channel_id=1, source_target_pairs={{0,1},{1,0},{2,3},{3,2},{4,5},{5,4},{6,7},{7,6},{8,9},{9,8},{10,11... | collective-permute-start | bytes 196616 | tf_op jit(solution)/shard_map/ppermute | solution.py:366
  98.5 9.4 %powers.1 = (f32[3,8,1024]{2,1,0:T(8,128)S(1)}, f32[3,8,1024]{2,1,0:T(8,128)S(1)}, f32[3,8,1024]{2,1,0:T(8,128)S(1)}) custom-call(s32[2]{0:T(128)S(1)} %pad_add_fusion.pos, f32[2,8,1024]{2,1,0:T(8,128)S(1)} %get-tuple-element.9.own, f32[2,8,1024]{2,1,0:T(8,128)S(1)} %collective-permute-done.6.sib, f32[2,8,1024]{2,1,0:T(8,128)S(1)} %collective-permute-done.7.near_a, ...), custom_call_target="tpu_custom_call" | custom-call | tf_op jit(solution)/shard_map/powers/pallas_call | solution.py:351
  107.9 3.5 %collective-permute-start.16 = (f32[3,8,1024]{2,1,0:T(8,128)S(1)}, f32[3,8,1024]{2,1,0:T(8,128)S(1)}, u32[]{:S(2)}, u32[]{:S(2)}) collective-permute-start(f32[3,8,1024]{2,1,0:T(8,128)S(1)} %get-tuple-element.10), channel_id=1, source_target_pairs={{0,128},{64,192},{128,256},{192,320},{256,384},{320,448},{1,129},{... | collective-permute-start | bytes 294920 | tf_op jit(solution)/shard_map/ppermute | solution.py:371
  111.4 2.0 %collective-permute-start.17 = (f32[3,8,1024]{2,1,0:T(8,128)S(1)}, f32[3,8,1024]{2,1,0:T(8,128)S(1)}, u32[]{:S(2)}, u32[]{:S(2)}) collective-permute-start(f32[3,8,1024]{2,1,0:T(8,128)S(1)} %get-tuple-element.11), channel_id=1, source_target_pairs={{0,256},{64,320},{128,384},{192,448},{1,257},{65,321},{129,385},{1... | collective-permute-start | bytes 294920 | tf_op jit(solution)/shard_map/ppermute | solution.py:371
  114.1 12.6 %collective-permute-start.20 = (f32[3,8,2048]{2,1,0:T(8,128)S(1)}, f32[3,8,2048]{2,1,0:T(8,128)S(1)}, u32[]{:S(2)}, u32[]{:S(2)}) collective-permute-start(f32[3,8,2048]{2,1,0:T(8,128)S(1)} %get-tuple-element.13), channel_id=1, source_target_pairs={{0,64},{64,128},{128,192},{192,256},{256,320},{320,384},{384,448},... | collective-permute-start | bytes 589832 | tf_op jit(solution)/shard_map/ppermute | solution.py:371
  126.8 2.0 %collective-permute-start.19 = (f32[3,8,1024]{2,1,0:T(8,128)S(1)}, f32[3,8,1024]{2,1,0:T(8,128)S(1)}, u32[]{:S(2)}, u32[]{:S(2)}) collective-permute-start(f32[3,8,1024]{2,1,0:T(8,128)S(1)} %add_add_fusion.own), channel_id=1, source_target_pairs={{0,64},{64,128},{128,192},{192,256},{256,320},{320,384},{384,448},... | collective-permute-start | bytes 294920 | tf_op jit(solution)/shard_map/ppermute | solution.py:371
  128.7 24.7 %collective-permute-done.20.detail = f32[3,8,2048]{2,1,0:T(8,128)S(1)} collective-permute-done((f32[3,8,2048]{2,1,0:T(8,128)S(1)}, f32[3,8,2048]{2,1,0:T(8,128)S(1)}, u32[]{:S(2)}, u32[]{:S(2)}) %collective-permute-start.20) | collective-permute-done | bytes 196640 | tf_op jit(solution)/shard_map/ppermute | solution.py:371
  153.4 2.0 %collective-permute-done.19.other = f32[3,8,1024]{2,1,0:T(8,128)S(1)} collective-permute-done((f32[3,8,1024]{2,1,0:T(8,128)S(1)}, f32[3,8,1024]{2,1,0:T(8,128)S(1)}, u32[]{:S(2)}, u32[]{:S(2)}) %collective-permute-start.19) | collective-permute-done | bytes 98336 | tf_op jit(solution)/shard_map/ppermute | solution.py:371
  (31 shorter events, 11.0 us)
Async XLA Ops:
  0.6 31.9 %copy-start = (f32[1,3,8,2048]{3,2,1,0:T(8,128)S(1)}, f32[1,3,8,2048]{3,2,1,0:T(8,128)}, u32[]{:S(2)}) copy-start(f32[1,3,8,2048]{3,2,1,0:T(8,128)} %param.2) | copy-start | bytes 589828
  0.6 31.9 %copy-start.2 = (f32[8,2048]{1,0:T(8,128)S(1)}, f32[8,2048]{1,0:T(8,128)}, u32[]{:S(2)}) copy-start(f32[8,2048]{1,0:T(8,128)} %field.3) | copy-start | bytes 196612
  1.7 17.1 %collective-permute-start.1 = (f32[4,8,2048]{2,1,0:T(8,128)S(1)}, f32[4,8,2048]{2,1,0:T(8,128)S(1)}, u32[]{:S(2)}, u32[]{:S(2)}) collective-permute-start(f32[4,8,2048]{2,1,0:T(8,128)S(1)} %pad_maximum_fusion), channel_id=1, source_target_pairs={{0,2},{1,3},{2,0},{3,1},{4,6},{5,7},{6,4},{7,5},{8,10},{9,11},{10,... | collective-permute-start | bytes 786440 | tf_op jit(solution)/shard_map/ppermute | solution.py:366
  5.5 21.4 %collective-permute-start = (f32[4,8,2048]{2,1,0:T(8,128)S(1)}, f32[4,8,2048]{2,1,0:T(8,128)S(1)}, u32[]{:S(2)}, u32[]{:S(2)}) collective-permute-start(f32[4,8,2048]{2,1,0:T(8,128)S(1)} %pad_maximum_fusion), channel_id=1, source_target_pairs={{2,4},{3,5},{4,2},{5,3},{6,8},{7,9},{8,6},{9,7},{10,12},{11,13},{1... | collective-permute-start | bytes 786440 | tf_op jit(solution)/shard_map/ppermute | solution.py:366
  16.8 15.6 %collective-permute-start.3 = (f32[4,8,2048]{2,1,0:T(8,128)S(1)}, f32[4,8,2048]{2,1,0:T(8,128)S(1)}, u32[]{:S(2)}, u32[]{:S(2)}) collective-permute-start(f32[4,8,2048]{2,1,0:T(8,128)S(1)} %pad_maximum_fusion), channel_id=1, source_target_pairs={{0,1},{1,0},{2,3},{3,2},{4,5},{5,4},{6,7},{7,6},{8,9},{9,8},{10,11... | collective-permute-start | bytes 786440 | tf_op jit(solution)/shard_map/ppermute | solution.py:366
  18.8 13.7 %collective-permute-start.5 = (f32[4,8,2048]{2,1,0:T(8,128)S(1)}, f32[4,8,2048]{2,1,0:T(8,128)S(1)}, u32[]{:S(2)}, u32[]{:S(2)}) collective-permute-start(f32[4,8,2048]{2,1,0:T(8,128)S(1)} %collective-permute-done.1.near_b), channel_id=1, source_target_pairs={{0,1},{1,0},{2,3},{3,2},{4,5},{5,4},{6,7},{7,6},{8,9},{9,8},{10,11... | collective-permute-start | bytes 786440 | tf_op jit(solution)/shard_map/ppermute | solution.py:366
  26.9 5.6 %collective-permute-start.4 = (f32[4,8,2048]{2,1,0:T(8,128)S(1)}, f32[4,8,2048]{2,1,0:T(8,128)S(1)}, u32[]{:S(2)}, u32[]{:S(2)}) collective-permute-start(f32[4,8,2048]{2,1,0:T(8,128)S(1)} %collective-permute-done.near_a), channel_id=1, source_target_pairs={{0,1},{1,0},{2,3},{3,2},{4,5},{5,4},{6,7},{7,6},{8,9},{9,8},{10,11... | collective-permute-start | bytes 786440 | tf_op jit(solution)/shard_map/ppermute | solution.py:366
  28.8 17.2 %collective-permute-start.2 = (f32[4,8,2048]{2,1,0:T(8,128)S(1)}, f32[4,8,2048]{2,1,0:T(8,128)S(1)}, u32[]{:S(2)}, u32[]{:S(2)}) collective-permute-start(f32[4,8,2048]{2,1,0:T(8,128)S(1)} %pad_maximum_fusion), channel_id=1, source_target_pairs={{1,4},{3,6},{4,1},{5,8},{6,3},{7,10},{8,5},{9,12},{10,7},{11,14},{... | collective-permute-start | bytes 786440 | tf_op jit(solution)/shard_map/ppermute | solution.py:366
  46.0 0.9 copy-start.1
  62.2 24.4 %collective-permute-start.15 = (f32[2,8,1024]{2,1,0:T(8,128)S(1)}, f32[2,8,1024]{2,1,0:T(8,128)S(1)}, u32[]{:S(2)}, u32[]{:S(2)}) collective-permute-start(f32[2,8,1024]{2,1,0:T(8,128)S(1)} %get-tuple-element.9.own), channel_id=1, source_target_pairs={{1,6},{3,8},{5,10},{6,1},{7,12},{8,3},{9,14},{10,5},{11,16},{12,7}... | collective-permute-start | bytes 196616 | tf_op jit(solution)/shard_map/ppermute | solution.py:366
  64.1 24.4 %collective-permute-start.13 = (f32[2,8,1024]{2,1,0:T(8,128)S(1)}, f32[2,8,1024]{2,1,0:T(8,128)S(1)}, u32[]{:S(2)}, u32[]{:S(2)}) collective-permute-start(f32[2,8,1024]{2,1,0:T(8,128)S(1)} %get-tuple-element.9.own), channel_id=1, source_target_pairs={{0,4},{1,5},{2,6},{3,7},{4,0},{5,1},{6,2},{7,3},{8,12},{9,13},{10,... | collective-permute-start | bytes 196616 | tf_op jit(solution)/shard_map/ppermute | solution.py:366
  70.8 20.2 %collective-permute-start.11 = (f32[2,8,1024]{2,1,0:T(8,128)S(1)}, f32[2,8,1024]{2,1,0:T(8,128)S(1)}, u32[]{:S(2)}, u32[]{:S(2)}) collective-permute-start(f32[2,8,1024]{2,1,0:T(8,128)S(1)} %get-tuple-element.9.own), channel_id=1, source_target_pairs={{4,8},{5,9},{6,10},{7,11},{8,4},{9,5},{10,6},{11,7},{12,16},{13,17... | collective-permute-start | bytes 196616 | tf_op jit(solution)/shard_map/ppermute | solution.py:366
  72.7 20.2 %collective-permute-start.9 = (f32[2,8,1024]{2,1,0:T(8,128)S(1)}, f32[2,8,1024]{2,1,0:T(8,128)S(1)}, u32[]{:S(2)}, u32[]{:S(2)}) collective-permute-start(f32[2,8,1024]{2,1,0:T(8,128)S(1)} %get-tuple-element.9.own), channel_id=1, source_target_pairs={{0,2},{1,3},{2,0},{3,1},{4,6},{5,7},{6,4},{7,5},{8,10},{9,11},{10,... | collective-permute-start | bytes 196616 | tf_op jit(solution)/shard_map/ppermute | solution.py:366
  74.6 20.7 %collective-permute-start.7 = (f32[2,8,1024]{2,1,0:T(8,128)S(1)}, f32[2,8,1024]{2,1,0:T(8,128)S(1)}, u32[]{:S(2)}, u32[]{:S(2)}) collective-permute-start(f32[2,8,1024]{2,1,0:T(8,128)S(1)} %get-tuple-element.9.own), channel_id=1, source_target_pairs={{2,4},{3,5},{4,2},{5,3},{6,8},{7,9},{8,6},{9,7},{10,12},{11,13},{1... | collective-permute-start | bytes 196616 | tf_op jit(solution)/shard_map/ppermute | solution.py:366
  86.6 10.7 %collective-permute-start.6 = (f32[2,8,1024]{2,1,0:T(8,128)S(1)}, f32[2,8,1024]{2,1,0:T(8,128)S(1)}, u32[]{:S(2)}, u32[]{:S(2)}) collective-permute-start(f32[2,8,1024]{2,1,0:T(8,128)S(1)} %get-tuple-element.9.own), channel_id=1, source_target_pairs={{0,1},{1,0},{2,3},{3,2},{4,5},{5,4},{6,7},{7,6},{8,9},{9,8},{10,11... | collective-permute-start | bytes 196616 | tf_op jit(solution)/shard_map/ppermute | solution.py:366
  88.5 8.7 %collective-permute-start.14 = (f32[2,8,1024]{2,1,0:T(8,128)S(1)}, f32[2,8,1024]{2,1,0:T(8,128)S(1)}, u32[]{:S(2)}, u32[]{:S(2)}) collective-permute-start(f32[2,8,1024]{2,1,0:T(8,128)S(1)} %collective-permute-done.13.far_b), channel_id=1, source_target_pairs={{0,1},{1,0},{2,3},{3,2},{4,5},{5,4},{6,7},{7,6},{8,9},{9,8},{10,11... | collective-permute-start | bytes 196616 | tf_op jit(solution)/shard_map/ppermute | solution.py:366
  91.0 6.3 %collective-permute-start.12 = (f32[2,8,1024]{2,1,0:T(8,128)S(1)}, f32[2,8,1024]{2,1,0:T(8,128)S(1)}, u32[]{:S(2)}, u32[]{:S(2)}) collective-permute-start(f32[2,8,1024]{2,1,0:T(8,128)S(1)} %collective-permute-done.11.far_a), channel_id=1, source_target_pairs={{0,1},{1,0},{2,3},{3,2},{4,5},{5,4},{6,7},{7,6},{8,9},{9,8},{10,11... | collective-permute-start | bytes 196616 | tf_op jit(solution)/shard_map/ppermute | solution.py:366
  92.9 4.4 %collective-permute-start.10 = (f32[2,8,1024]{2,1,0:T(8,128)S(1)}, f32[2,8,1024]{2,1,0:T(8,128)S(1)}, u32[]{:S(2)}, u32[]{:S(2)}) collective-permute-start(f32[2,8,1024]{2,1,0:T(8,128)S(1)} %collective-permute-done.9.near_b), channel_id=1, source_target_pairs={{0,1},{1,0},{2,3},{3,2},{4,5},{5,4},{6,7},{7,6},{8,9},{9,8},{10,11... | collective-permute-start | bytes 196616 | tf_op jit(solution)/shard_map/ppermute | solution.py:366
  95.3 3.1 %collective-permute-start.8 = (f32[2,8,1024]{2,1,0:T(8,128)S(1)}, f32[2,8,1024]{2,1,0:T(8,128)S(1)}, u32[]{:S(2)}, u32[]{:S(2)}) collective-permute-start(f32[2,8,1024]{2,1,0:T(8,128)S(1)} %collective-permute-done.7.near_a), channel_id=1, source_target_pairs={{0,1},{1,0},{2,3},{3,2},{4,5},{5,4},{6,7},{7,6},{8,9},{9,8},{10,11... | collective-permute-start | bytes 196616 | tf_op jit(solution)/shard_map/ppermute | solution.py:366
  107.9 18.8 %collective-permute-start.16 = (f32[3,8,1024]{2,1,0:T(8,128)S(1)}, f32[3,8,1024]{2,1,0:T(8,128)S(1)}, u32[]{:S(2)}, u32[]{:S(2)}) collective-permute-start(f32[3,8,1024]{2,1,0:T(8,128)S(1)} %get-tuple-element.10), channel_id=1, source_target_pairs={{0,128},{64,192},{128,256},{192,320},{256,384},{320,448},{1,129},{... | collective-permute-start | bytes 294920 | tf_op jit(solution)/shard_map/ppermute | solution.py:371
  111.4 15.3 %collective-permute-start.17 = (f32[3,8,1024]{2,1,0:T(8,128)S(1)}, f32[3,8,1024]{2,1,0:T(8,128)S(1)}, u32[]{:S(2)}, u32[]{:S(2)}) collective-permute-start(f32[3,8,1024]{2,1,0:T(8,128)S(1)} %get-tuple-element.11), channel_id=1, source_target_pairs={{0,256},{64,320},{128,384},{192,448},{1,257},{65,321},{129,385},{1... | collective-permute-start | bytes 294920 | tf_op jit(solution)/shard_map/ppermute | solution.py:371
  113.4 13.3 %collective-permute-start.18 = (f32[3,8,1024]{2,1,0:T(8,128)S(1)}, f32[3,8,1024]{2,1,0:T(8,128)S(1)}, u32[]{:S(2)}, u32[]{:S(2)}) collective-permute-start(f32[3,8,1024]{2,1,0:T(8,128)S(1)} %get-tuple-element.12), channel_id=1, source_target_pairs={{0,384},{64,448},{1,385},{65,449},{2,386},{66,450},{3,387},{67,451... | collective-permute-start | bytes 294920 | tf_op jit(solution)/shard_map/ppermute | solution.py:371
  114.1 39.3 %collective-permute-start.20 = (f32[3,8,2048]{2,1,0:T(8,128)S(1)}, f32[3,8,2048]{2,1,0:T(8,128)S(1)}, u32[]{:S(2)}, u32[]{:S(2)}) collective-permute-start(f32[3,8,2048]{2,1,0:T(8,128)S(1)} %get-tuple-element.13), channel_id=1, source_target_pairs={{0,64},{64,128},{128,192},{192,256},{256,320},{320,384},{384,448},... | collective-permute-start | bytes 589832 | tf_op jit(solution)/shard_map/ppermute | solution.py:371
  126.8 28.7 %collective-permute-start.19 = (f32[3,8,1024]{2,1,0:T(8,128)S(1)}, f32[3,8,1024]{2,1,0:T(8,128)S(1)}, u32[]{:S(2)}, u32[]{:S(2)}) collective-permute-start(f32[3,8,1024]{2,1,0:T(8,128)S(1)} %add_add_fusion.own), channel_id=1, source_target_pairs={{0,64},{64,128},{128,192},{192,256},{256,320},{320,384},{384,448},... | collective-permute-start | bytes 294920 | tf_op jit(solution)/shard_map/ppermute | solution.py:371
where the time goes:
time: 158 us; the launch traced here: 157 us
  starting transfers between devices  80.6 us (51%)
  waiting for transfers between devices  44.7 us (28%)
  Pallas kernels  28.4 us (18%)
    ppermute x16, starting transfers between devices, swap(): return lax.ppermute(block, 'space', pairs)  59.9 us
    pallas_call x4, Pallas kernels, call(): pl.pallas_call(kernel, out_shape=outs, in_specs=[SMEM] + [VMEM] * (len(ar...  28.4 us
    ppermute x5, waiting for transfers between devices, later(): lax.ppermute(block, 'tm', [(m, m + distance) for m in range(slices - dist...  26.7 us
    ppermute x5, starting transfers between devices, later(): lax.ppermute(block, 'tm', [(m, m + distance) for m in range(slices - dist...  20.7 us
    ppermute x16, waiting for transfers between devices, swap(): return lax.ppermute(block, 'space', pairs)  18 us
  transfers between devices with their start and end apart: 21, of which 5 were waited for; matrix products, arithmetic and copies ran while one was open for 0% of the time, Pallas kernels for 2%

commit v1 on v0

--- a/solution.py
+++ b/solution.py
@@ -231,11 +231,12 @@
         means = []
         for comp in range(3):
             sides = []
-            for s in (k, k + half):
+            both = unfolded(coarse[comp, :, pl.ds(k * LANES, LANES)], lane)
+            for s, less in zip((k, k + half), both):
                 lanes = pl.ds(s * LANES, LANES)
                 value = a[3, comp, :, strip(s)]
                 out[comp, :, lanes] = value
-                rest = value - keep * coarse[comp, :, lanes]
+                rest = value - keep * less
                 detail[comp, :, lanes] = rest
                 sides.append(pair_mean(rest, sub, lane))
             means.append(folded(*sides, lane))
@@ -254,7 +255,9 @@
     run(one, three, weight=1.0, length=length, tiles=tiles_of(2))
 
 
-def coarse_kernel(count, strips, pos, state, field, sib, sib_a, sib_b, out, one, two, three, window):
+def coarse_kernel(
+    count, strips, pos, state, field, sib, sib_a, sib_b, out, short, one, two, three, window
+):
     position = pos[0]
     side, near, _ = places(position)
     sub, lane = iotas()
@@ -283,13 +286,14 @@
     coarse_step((one, two, three), window, lambda n: range(3) if n < 2 else (1,), half, GROUP)
     for k in range(half):
         for comp in range(3):
-            for s, value in zip((k, k + half), unfolded(one[1, comp, :, strip(k)], lane)):
-                out[comp, :, pl.ds(s * LANES, LANES)] = value
+            value = one[1, comp, :, strip(k)]
+            short[comp, :, pl.ds(k * LANES, LANES)] = value
+            for s, part in zip((k, k + half), unfolded(value, lane)):
+                out[comp, :, pl.ds(s * LANES, LANES)] = part
 
 
 def powers_kernel(
-    count, strips, pos, own, sib, near_a, sib_a, near_b, sib_b, far_a, far_sa, far_b, far_sb, fifth,
-    *refs,
+    count, strips, pos, own, sib, near_a, near_b, far_a, far_b, fifth, others, *refs
 ):
     outs, (one, two, three, window) = refs[:3], refs[3:]
     position = pos[0]
@@ -297,16 +301,16 @@
     sub, lane = iotas()
     half = strips // 2
     arrived = (
-        (own, 0), (sib, side), (near_a, near), (sib_a, near + side), (near_b, -near),
-        (sib_b, side - near), (far_a, far), (far_sa, far + side), (far_b, -far),
-        (far_sb, side - far), (fifth, -5 * side),
-    )
-    for ref, offset in arrived:
+        (own, 0, 0), (sib, 0, side), (near_a, 0, near), (near_b, 0, -near), (far_a, 0, far),
+        (far_b, 0, -far), (fifth, 0, -5 * side), (others, 0, near + side),
+        (others, 2, side - near), (others, 4, far + side), (others, 6, side - far),
+    )
+    for ref, at, offset in arrived:
         slot = 5 + offset
         for k in range(half):
             lanes = pl.ds(k * LANES, LANES)
-            height, east = unzipped(ref[0, :, lanes], sub)
-            north, plane = unzipped(ref[1, :, lanes], sub)
+            height, east = unzipped(ref[at, :, lanes], sub)
+            north, plane = unzipped(ref[at + 1, :, lanes], sub)
             one[slot, 0, :, strip(k)] = height
             one[slot, 1, :, strip(k)] = east
             one[slot, 2, :, strip(k)] = north
@@ -338,8 +342,8 @@
     first = pos[1] == 0
     for k in range(half):
         lanes = pl.ds(k * LANES, LANES)
-        height, east = unzipped(own[0, :, lanes] + other[1, :, lanes], sub)
-        north = unzipped(own[2, :, lanes], sub)[0] + unzipped(other[2, :, lanes], sub)[1]
+        height, east = unzipped(own[0, :, lanes] + other[0, :, lanes], sub)
+        north = unzipped(own[2, :, lanes], sub)[0] + unzipped(other[1, :, lanes], sub)[1]
         for comp, value in enumerate((height, east, north)):
             for s, part in zip((k, k + half), unfolded(value, lane)):
                 wide = pl.ds(s * LANES, LANES)
@@ -371,6 +375,24 @@
     return lax.ppermute(block, "tm", [(m, m + distance) for m in range(slices - distance)])
 
 
+def in_two_legs(block):
+    slices, count = lax.axis_size("tm"), lax.axis_size("space")
+    run = min(8, count // 2)
+    legs = [], []
+    for m in range(slices - 1):
+        for i in range(count):
+            y, upper = divmod(m, 2)
+            group, low = divmod(i // 2, run)
+            way = 1 if i % 2 == 0 else -1
+            upper, low = divmod((upper * run + low + way * (run // 2)) % (2 * run), run)
+            stop = (2 * y + upper) * count + 2 * (group * run + low) + i % 2
+            legs[0].append((m * count + i, stop))
+            legs[1].append((stop, (m + 1) * count + i))
+    for leg in legs:
+        block = lax.ppermute(block, ("tm", "space"), leg)
+    return block
+
+
 def sibling(i):
     return i + 1 - 2 * (i % 2)
 
@@ -415,10 +437,11 @@
     b = swap(sent, near_even)
     q = swap(sent, third)
     a = swap(sent, near_odd)
+    a, b, q = lax.optimization_barrier((a, b, q))
     sib_b, sib_a = swap(b, sibling), swap(a, sibling)
-    (coarse_end,) = call(
+    coarse_end, short = call(
         functools.partial(coarse_kernel, count, strips),
-        [tile],
+        [tile, shape(3, ROWS, cols // 2)],
         [buf(3, cols // 2)] * 3 + [plane(3, cols // 2)],
         "coarse",
         pos, state, vertical_field, sib, sib_a, sib_b,
@@ -428,25 +451,26 @@
         [tile, tile, shape(2, ROWS, cols // 2)],
         [buf(7, cols), buf(7, cols), plane(7, cols)],
         "fine",
-        pos, state, vertical_field, a, b, q, sib, sib_a, sib_b, coarse_end,
-    )
-    arrived = later(detail, 1)
+        pos, state, vertical_field, a, b, q, sib, sib_a, sib_b, short,
+    )
+    arrived = in_two_legs(detail)
     sib = swap(message, sibling)
     b = swap(message, near_even)
     d = swap(message, far_even)
     q = swap(message, fifth)
     c = swap(message, far_odd)
     a = swap(message, near_odd)
-    sib_b, sib_d, sib_c, sib_a = [swap(x, sibling) for x in (b, d, c, a)]
+    a, b, c, d, q = lax.optimization_barrier((a, b, c, d, q))
+    others = swap(jnp.concatenate([a, b, c, d], axis=0), sibling)
     powers = call(
         functools.partial(powers_kernel, count, strips),
         [shape(3, ROWS, cols // 2)] * 3,
         [buf(11, cols // 2)] * 3 + [plane(11, cols // 2)],
         "powers",
-        pos, message, sib, a, sib_a, b, sib_b, c, sib_c, d, sib_d, q,
+        pos, message, sib, a, b, c, d, q, others,
     )
     own = sum(later(x, 2 * d + 2) for d, x in enumerate(powers))
-    other = later(own, 1)
+    other = later(own[1:], 1)
     (new_start,) = call(
         functools.partial(final_kernel, strips),
         [tile],

time: 158 us -> 143 us (0.905)
  waiting for transfers between devices: 44.7 us -> 30.1 us
    ppermute x5 -> x4, waiting for transfers between devices: 26.7 us -> 8.07 us  [later(): lax.ppermute(block, 'tm', [(m, m + distance) for m in range(slices - dist...]
    ppermute x0 -> x2, starting transfers between devices: none -> 15.1 us  [in_two_legs(): block = lax.ppermute(block, ('tm', 'space'), leg)]
    ppermute x5 -> x4, starting transfers between devices: 20.7 us -> 12.6 us  [later(): lax.ppermute(block, 'tm', [(m, m + distance) for m in range(slices - dist...]
    ppermute x16 -> x13, starting transfers between devices: 59.9 us -> 53.3 us  [swap(): return lax.ppermute(block, 'space', pairs)]
    ppermute x0 -> x2, waiting for transfers between devices: none -> 3.89 us  [in_two_legs(): block = lax.ppermute(block, ('tm', 'space'), leg)]
    ppermute x16 -> x13, waiting for transfers between devices: 18 us -> 18.2 us  [swap(): return lax.ppermute(block, 'space', pairs)]
  transfers between devices with their start and end apart: 21 -> 19, of which waited for: 5 -> 7; matrix products, arithmetic and copies ran while one was open for 0% -> 0% of each run, Pallas kernels for 2% -> 7%
where the time goes in v1:
time: 143 us; the launch traced here: 142 us
  starting transfers between devices  81 us (57%)
  waiting for transfers between devices  30.1 us (21%)
  Pallas kernels  28.9 us (20%)
    ppermute x13, starting transfers between devices, swap(): return lax.ppermute(block, 'space', pairs)  53.3 us
    pallas_call x4, Pallas kernels, call(): pl.pallas_call(kernel, out_shape=outs, in_specs=[SMEM] + [VMEM] * (len(ar...  28.9 us
    ppermute x13, waiting for transfers between devices, swap(): return lax.ppermute(block, 'space', pairs)  18.2 us
    ppermute x2, starting transfers between devices, in_two_legs(): block = lax.ppermute(block, ('tm', 'space'), leg)  15.1 us
    ppermute x4, starting transfers between devices, later(): lax.ppermute(block, 'tm', [(m, m + distance) for m in range(slices - dist...  12.6 us
    ppermute x4, waiting for transfers between devices, later(): lax.ppermute(block, 'tm', [(m, m + distance) for m in range(slices - dist...  8.07 us
    ppermute x2, waiting for transfers between devices, in_two_legs(): block = lax.ppermute(block, ('tm', 'space'), leg)  3.89 us
  transfers between devices with their start and end apart: 19, of which 7 were waited for; matrix products, arithmetic and copies ran while one was open for 0% of the time, Pallas kernels for 7%

profile of v1, /device:TPU:10, one launch (start us, length us, event | category | flops | bytes accessed | tf_op | source)
XLA Modules:
  0.0 142.1 jit_solution(5365413813222950179)
XLA Ops:
  1.7 11.2 %collective-permute-start.2 = (f32[4,8,2048]{2,1,0:T(8,128)S(1)}, f32[4,8,2048]{2,1,0:T(8,128)S(1)}, u32[]{:S(2)}, u32[]{:S(2)}) collective-permute-start(f32[4,8,2048]{2,1,0:T(8,128)S(1)} %pad_maximum_fusion), channel_id=1, source_target_pairs={{1,4},{3,6},{4,1},{5,8},{6,3},{7,10},{8,5},{9,12},{10,7},{11,14},{... | collective-permute-start | bytes 786440 | tf_op jit(solution)/shard_map/ppermute | solution.py:370
  12.9 3.8 %collective-permute-start.1 = (f32[4,8,2048]{2,1,0:T(8,128)S(1)}, f32[4,8,2048]{2,1,0:T(8,128)S(1)}, u32[]{:S(2)}, u32[]{:S(2)}) collective-permute-start(f32[4,8,2048]{2,1,0:T(8,128)S(1)} %pad_maximum_fusion), channel_id=1, source_target_pairs={{0,2},{1,3},{2,0},{3,1},{4,6},{5,7},{6,4},{7,5},{8,10},{9,11},{10,... | collective-permute-start | bytes 786440 | tf_op jit(solution)/shard_map/ppermute | solution.py:370
  16.7 2.0 %collective-permute-start = (f32[4,8,2048]{2,1,0:T(8,128)S(1)}, f32[4,8,2048]{2,1,0:T(8,128)S(1)}, u32[]{:S(2)}, u32[]{:S(2)}) collective-permute-start(f32[4,8,2048]{2,1,0:T(8,128)S(1)} %pad_maximum_fusion), channel_id=1, source_target_pairs={{2,4},{3,5},{4,2},{5,3},{6,8},{7,9},{8,6},{9,7},{10,12},{11,13},{1... | collective-permute-start | bytes 786440 | tf_op jit(solution)/shard_map/ppermute | solution.py:370
  18.8 1.9 %collective-permute-start.3 = (f32[4,8,2048]{2,1,0:T(8,128)S(1)}, f32[4,8,2048]{2,1,0:T(8,128)S(1)}, u32[]{:S(2)}, u32[]{:S(2)}) collective-permute-start(f32[4,8,2048]{2,1,0:T(8,128)S(1)} %pad_maximum_fusion), channel_id=1, source_target_pairs={{0,1},{1,0},{2,3},{3,2},{4,5},{5,4},{6,7},{7,6},{8,9},{9,8},{10,11... | collective-permute-start | bytes 786440 | tf_op jit(solution)/shard_map/ppermute | solution.py:370
  20.7 3.9 %collective-permute-done.2.third = f32[4,8,2048]{2,1,0:T(8,128)S(1)} collective-permute-done((f32[4,8,2048]{2,1,0:T(8,128)S(1)}, f32[4,8,2048]{2,1,0:T(8,128)S(1)}, u32[]{:S(2)}, u32[]{:S(2)}) %collective-permute-start.2) | collective-permute-done | bytes 262176 | tf_op jit(solution)/shard_map/ppermute | solution.py:370
  24.6 8.0 %collective-permute-done.near_a = f32[4,8,2048]{2,1,0:T(8,128)S(1)} collective-permute-done((f32[4,8,2048]{2,1,0:T(8,128)S(1)}, f32[4,8,2048]{2,1,0:T(8,128)S(1)}, u32[]{:S(2)}, u32[]{:S(2)}) %collective-permute-start) | collective-permute-done | bytes 262176 | tf_op jit(solution)/shard_map/ppermute | solution.py:370
  34.6 2.4 %collective-permute-start.5 = (f32[4,8,2048]{2,1,0:T(8,128)S(1)}, f32[4,8,2048]{2,1,0:T(8,128)S(1)}, u32[]{:S(2)}, u32[]{:S(2)}) collective-permute-start(f32[4,8,2048]{2,1,0:T(8,128)S(1)} %collective-permute-done.1.near_b), channel_id=1, source_target_pairs={{0,1},{1,0},{2,3},{3,2},{4,5},{5,4},{6,7},{7,6},{8,9},{9,8},{10,11... | collective-permute-start | bytes 786440 | tf_op jit(solution)/shard_map/ppermute | solution.py:370
  38.1 2.4 %coarse.1 = (f32[3,8,2048]{2,1,0:T(8,128)}, f32[3,8,1024]{2,1,0:T(8,128)S(1)}) custom-call(s32[2]{0:T(128)S(1)} %pad_add_fusion.pos, f32[3,8,2048]{2,1,0:T(8,128)S(1)} %bitcast.8, f32[8,2048]{1,0:T(8,128)S(1)} %copy-done.1, f32[4,8,2048]{2,1,0:T(8,128)S(1)} %collective-permute-done.3.sib, f32[4,8,2048]{2,1,0:T(8,128)S(1)} %collective-permute-done.4.sib_a, ...), custom_call_target="tpu_custom_call" | custom-call | tf_op jit(solution)/shard_map/coarse/pallas_call | solution.py:355
  40.6 15.7 %fine.1 = (f32[3,8,2048]{2,1,0:T(8,128)}, f32[3,8,2048]{2,1,0:T(8,128)S(1)}, f32[2,8,1024]{2,1,0:T(8,128)S(1)}) custom-call(s32[2]{0:T(128)S(1)} %pad_add_fusion.pos, f32[3,8,2048]{2,1,0:T(8,128)S(1)} %bitcast.9, f32[8,2048]{1,0:T(8,128)S(1)} %copy-done.1, f32[4,8,2048]{2,1,0:T(8,128)S(1)} %collective-permute-done.near_a, ...), custom_call_target="tpu_custom_call" | custom-call | tf_op jit(solution)/shard_map/fine/pallas_call | solution.py:355
  56.2 6.5 %collective-permute-start.11 = (f32[2,8,1024]{2,1,0:T(8,128)S(1)}, f32[2,8,1024]{2,1,0:T(8,128)S(1)}, u32[]{:S(2)}, u32[]{:S(2)}) collective-permute-start(f32[2,8,1024]{2,1,0:T(8,128)S(1)} %get-tuple-element.23.own), channel_id=1, source_target_pairs={{1,6},{3,8},{5,10},{6,1},{7,12},{8,3},{9,14},{10,5},{11,16},{12,7}... | collective-permute-start | bytes 196616 | tf_op jit(solution)/shard_map/ppermute | solution.py:370
  62.7 2.6 %collective-permute-start.10 = (f32[2,8,1024]{2,1,0:T(8,128)S(1)}, f32[2,8,1024]{2,1,0:T(8,128)S(1)}, u32[]{:S(2)}, u32[]{:S(2)}) collective-permute-start(f32[2,8,1024]{2,1,0:T(8,128)S(1)} %get-tuple-element.23.own), channel_id=1, source_target_pairs={{0,4},{1,5},{2,6},{3,7},{4,0},{5,1},{6,2},{7,3},{8,12},{9,13},{10,... | collective-permute-start | bytes 196616 | tf_op jit(solution)/shard_map/ppermute | solution.py:370
  65.3 3.7 %collective-permute-start.9 = (f32[2,8,1024]{2,1,0:T(8,128)S(1)}, f32[2,8,1024]{2,1,0:T(8,128)S(1)}, u32[]{:S(2)}, u32[]{:S(2)}) collective-permute-start(f32[2,8,1024]{2,1,0:T(8,128)S(1)} %get-tuple-element.23.own), channel_id=1, source_target_pairs={{4,8},{5,9},{6,10},{7,11},{8,4},{9,5},{10,6},{11,7},{12,16},{13,17... | collective-permute-start | bytes 196616 | tf_op jit(solution)/shard_map/ppermute | solution.py:370
  69.1 2.7 %collective-permute-start.8 = (f32[2,8,1024]{2,1,0:T(8,128)S(1)}, f32[2,8,1024]{2,1,0:T(8,128)S(1)}, u32[]{:S(2)}, u32[]{:S(2)}) collective-permute-start(f32[2,8,1024]{2,1,0:T(8,128)S(1)} %get-tuple-element.23.own), channel_id=1, source_target_pairs={{0,2},{1,3},{2,0},{3,1},{4,6},{5,7},{6,4},{7,5},{8,10},{9,11},{10,... | collective-permute-start | bytes 196616 | tf_op jit(solution)/shard_map/ppermute | solution.py:370
  71.8 9.4 %collective-permute-start.7 = (f32[2,8,1024]{2,1,0:T(8,128)S(1)}, f32[2,8,1024]{2,1,0:T(8,128)S(1)}, u32[]{:S(2)}, u32[]{:S(2)}) collective-permute-start(f32[2,8,1024]{2,1,0:T(8,128)S(1)} %get-tuple-element.23.own), channel_id=1, source_target_pairs={{2,4},{3,5},{4,2},{5,3},{6,8},{7,9},{8,6},{9,7},{10,12},{11,13},{1... | collective-permute-start | bytes 196616 | tf_op jit(solution)/shard_map/ppermute | solution.py:370
  81.2 4.2 %collective-permute-done.7.near_a = f32[2,8,1024]{2,1,0:T(8,128)S(1)} collective-permute-done((f32[2,8,1024]{2,1,0:T(8,128)S(1)}, f32[2,8,1024]{2,1,0:T(8,128)S(1)}, u32[]{:S(2)}, u32[]{:S(2)}) %collective-permute-start.7) | collective-permute-done | bytes 65568 | tf_op jit(solution)/shard_map/ppermute | solution.py:370
  85.4 2.9 %collective-permute-start.12 = (f32[8,8,1024]{2,1,0:T(8,128)S(1)}, f32[8,8,1024]{2,1,0:T(8,128)S(1)}, u32[]{:S(2)}, u32[]{:S(2)}) collective-permute-start(f32[8,8,1024]{2,1,0:T(8,128)S(1)} %pad_maximum_fusion.1), channel_id=1, source_target_pairs={{0,1},{1,0},{2,3},{3,2},{4,5},{5,4},{6,7},{7,6},{8,9},{9,8},{10,11... | collective-permute-start | bytes 786440 | tf_op jit(solution)/shard_map/ppermute | solution.py:370
  90.2 2.2 %collective-permute-start.6 = (f32[2,8,1024]{2,1,0:T(8,128)S(1)}, f32[2,8,1024]{2,1,0:T(8,128)S(1)}, u32[]{:S(2)}, u32[]{:S(2)}) collective-permute-start(f32[2,8,1024]{2,1,0:T(8,128)S(1)} %get-tuple-element.23.own), channel_id=1, source_target_pairs={{0,1},{1,0},{2,3},{3,2},{4,5},{5,4},{6,7},{7,6},{8,9},{9,8},{10,11... | collective-permute-start | bytes 196616 | tf_op jit(solution)/shard_map/ppermute | solution.py:370
  93.4 9.4 %powers.1 = (f32[3,8,1024]{2,1,0:T(8,128)S(1)}, f32[3,8,1024]{2,1,0:T(8,128)S(1)}, f32[3,8,1024]{2,1,0:T(8,128)S(1)}) custom-call(s32[2]{0:T(128)S(1)} %pad_add_fusion.pos, f32[2,8,1024]{2,1,0:T(8,128)S(1)} %get-tuple-element.23.own, f32[2,8,1024]{2,1,0:T(8,128)S(1)} %collective-permute-done.6.sib, f32[2,8,1024]{2,1,0:T(8,128)S(1)} %collective-permute-done.7.near_a, ...), custom_call_target="tpu_custom_call" | custom-call | tf_op jit(solution)/shard_map/powers/pallas_call | solution.py:355
  102.8 3.5 %collective-permute-start.13 = (f32[3,8,1024]{2,1,0:T(8,128)S(1)}, f32[3,8,1024]{2,1,0:T(8,128)S(1)}, u32[]{:S(2)}, u32[]{:S(2)}) collective-permute-start(f32[3,8,1024]{2,1,0:T(8,128)S(1)} %get-tuple-element.29), channel_id=1, source_target_pairs={{0,128},{64,192},{128,256},{192,320},{256,384},{320,448},{1,129},{... | collective-permute-start | bytes 294920 | tf_op jit(solution)/shard_map/ppermute | solution.py:375
  106.3 2.0 %collective-permute-start.14 = (f32[3,8,1024]{2,1,0:T(8,128)S(1)}, f32[3,8,1024]{2,1,0:T(8,128)S(1)}, u32[]{:S(2)}, u32[]{:S(2)}) collective-permute-start(f32[3,8,1024]{2,1,0:T(8,128)S(1)} %get-tuple-element.30), channel_id=1, source_target_pairs={{0,256},{64,320},{128,384},{192,448},{1,257},{65,321},{129,385},{1... | collective-permute-start | bytes 294920 | tf_op jit(solution)/shard_map/ppermute | solution.py:375
  109.0 13.2 %collective-permute-start.18 = (f32[3,8,2048]{2,1,0:T(8,128)S(1)}, f32[3,8,2048]{2,1,0:T(8,128)S(1)}, u32[]{:S(2)}, u32[]{:S(2)}) collective-permute-start(f32[3,8,2048]{2,1,0:T(8,128)S(1)} %collective-permute-done.17), channel_id=1, source_target_pairs={{8,64},{73,65},{10,66},{75,67},{12,68},{77,69},{14,70},{79,71},{64... | collective-permute-start | bytes 589832 | tf_op jit(solution)/shard_map/ppermute | solution.py:392
  122.3 6.5 %collective-permute-start.16 = (f32[2,8,1024]{2,1,0:T(8,128)S(1)}, f32[2,8,1024]{2,1,0:T(8,128)S(1)}, u32[]{:S(2)}, u32[]{:S(2)}) collective-permute-start(f32[2,8,1024]{2,1,0:T(8,128)S(1)} %slice.4), channel_id=1, source_target_pairs={{0,64},{64,128},{128,192},{192,256},{256,320},{320,384},{384,448},... | collective-permute-start | bytes 196616 | tf_op jit(solution)/shard_map/ppermute | solution.py:375
  128.8 3.9 %collective-permute-done.18.detail = f32[3,8,2048]{2,1,0:T(8,128)S(1)} collective-permute-done((f32[3,8,2048]{2,1,0:T(8,128)S(1)}, f32[3,8,2048]{2,1,0:T(8,128)S(1)}, u32[]{:S(2)}, u32[]{:S(2)}) %collective-permute-start.18) | collective-permute-done | bytes 196640 | tf_op jit(solution)/shard_map/ppermute | solution.py:392
  132.7 8.1 %collective-permute-done.16.other = f32[2,8,1024]{2,1,0:T(8,128)S(1)} collective-permute-done((f32[2,8,1024]{2,1,0:T(8,128)S(1)}, f32[2,8,1024]{2,1,0:T(8,128)S(1)}, u32[]{:S(2)}, u32[]{:S(2)}) %collective-permute-start.16) | collective-permute-done | bytes 65568 | tf_op jit(solution)/shard_map/ppermute | solution.py:375
  (27 shorter events, 9.0 us)
Async XLA Ops:
  0.6 37.5 %copy-start = (f32[1,3,8,2048]{3,2,1,0:T(8,128)S(1)}, f32[1,3,8,2048]{3,2,1,0:T(8,128)}, u32[]{:S(2)}) copy-start(f32[1,3,8,2048]{3,2,1,0:T(8,128)} %param.2) | copy-start | bytes 589828
  0.6 37.5 %copy-start.1 = (f32[8,2048]{1,0:T(8,128)S(1)}, f32[8,2048]{1,0:T(8,128)}, u32[]{:S(2)}) copy-start(f32[8,2048]{1,0:T(8,128)} %field.3) | copy-start | bytes 196612
  1.7 23.0 %collective-permute-start.2 = (f32[4,8,2048]{2,1,0:T(8,128)S(1)}, f32[4,8,2048]{2,1,0:T(8,128)S(1)}, u32[]{:S(2)}, u32[]{:S(2)}) collective-permute-start(f32[4,8,2048]{2,1,0:T(8,128)S(1)} %pad_maximum_fusion), channel_id=1, source_target_pairs={{1,4},{3,6},{4,1},{5,8},{6,3},{7,10},{8,5},{9,12},{10,7},{11,14},{... | collective-permute-start | bytes 786440 | tf_op jit(solution)/shard_map/ppermute | solution.py:370
  12.9 11.7 %collective-permute-start.1 = (f32[4,8,2048]{2,1,0:T(8,128)S(1)}, f32[4,8,2048]{2,1,0:T(8,128)S(1)}, u32[]{:S(2)}, u32[]{:S(2)}) collective-permute-start(f32[4,8,2048]{2,1,0:T(8,128)S(1)} %pad_maximum_fusion), channel_id=1, source_target_pairs={{0,2},{1,3},{2,0},{3,1},{4,6},{5,7},{6,4},{7,5},{8,10},{9,11},{10,... | collective-permute-start | bytes 786440 | tf_op jit(solution)/shard_map/ppermute | solution.py:370
  16.7 15.9 %collective-permute-start = (f32[4,8,2048]{2,1,0:T(8,128)S(1)}, f32[4,8,2048]{2,1,0:T(8,128)S(1)}, u32[]{:S(2)}, u32[]{:S(2)}) collective-permute-start(f32[4,8,2048]{2,1,0:T(8,128)S(1)} %pad_maximum_fusion), channel_id=1, source_target_pairs={{2,4},{3,5},{4,2},{5,3},{6,8},{7,9},{8,6},{9,7},{10,12},{11,13},{1... | collective-permute-start | bytes 786440 | tf_op jit(solution)/shard_map/ppermute | solution.py:370
  18.8 18.3 %collective-permute-start.3 = (f32[4,8,2048]{2,1,0:T(8,128)S(1)}, f32[4,8,2048]{2,1,0:T(8,128)S(1)}, u32[]{:S(2)}, u32[]{:S(2)}) collective-permute-start(f32[4,8,2048]{2,1,0:T(8,128)S(1)} %pad_maximum_fusion), channel_id=1, source_target_pairs={{0,1},{1,0},{2,3},{3,2},{4,5},{5,4},{6,7},{7,6},{8,9},{9,8},{10,11... | collective-permute-start | bytes 786440 | tf_op jit(solution)/shard_map/ppermute | solution.py:370
  32.7 4.4 %collective-permute-start.4 = (f32[4,8,2048]{2,1,0:T(8,128)S(1)}, f32[4,8,2048]{2,1,0:T(8,128)S(1)}, u32[]{:S(2)}, u32[]{:S(2)}) collective-permute-start(f32[4,8,2048]{2,1,0:T(8,128)S(1)} %collective-permute-done.near_a), channel_id=1, source_target_pairs={{0,1},{1,0},{2,3},{3,2},{4,5},{5,4},{6,7},{7,6},{8,9},{9,8},{10,11... | collective-permute-start | bytes 786440 | tf_op jit(solution)/shard_map/ppermute | solution.py:370
  34.6 3.6 %collective-permute-start.5 = (f32[4,8,2048]{2,1,0:T(8,128)S(1)}, f32[4,8,2048]{2,1,0:T(8,128)S(1)}, u32[]{:S(2)}, u32[]{:S(2)}) collective-permute-start(f32[4,8,2048]{2,1,0:T(8,128)S(1)} %collective-permute-done.1.near_b), channel_id=1, source_target_pairs={{0,1},{1,0},{2,3},{3,2},{4,5},{5,4},{6,7},{7,6},{8,9},{9,8},{10,11... | collective-permute-start | bytes 786440 | tf_op jit(solution)/shard_map/ppermute | solution.py:370
  56.2 24.9 %collective-permute-start.11 = (f32[2,8,1024]{2,1,0:T(8,128)S(1)}, f32[2,8,1024]{2,1,0:T(8,128)S(1)}, u32[]{:S(2)}, u32[]{:S(2)}) collective-permute-start(f32[2,8,1024]{2,1,0:T(8,128)S(1)} %get-tuple-element.23.own), channel_id=1, source_target_pairs={{1,6},{3,8},{5,10},{6,1},{7,12},{8,3},{9,14},{10,5},{11,16},{12,7}... | collective-permute-start | bytes 196616 | tf_op jit(solution)/shard_map/ppermute | solution.py:370
  62.7 18.5 %collective-permute-start.10 = (f32[2,8,1024]{2,1,0:T(8,128)S(1)}, f32[2,8,1024]{2,1,0:T(8,128)S(1)}, u32[]{:S(2)}, u32[]{:S(2)}) collective-permute-start(f32[2,8,1024]{2,1,0:T(8,128)S(1)} %get-tuple-element.23.own), channel_id=1, source_target_pairs={{0,4},{1,5},{2,6},{3,7},{4,0},{5,1},{6,2},{7,3},{8,12},{9,13},{10,... | collective-permute-start | bytes 196616 | tf_op jit(solution)/shard_map/ppermute | solution.py:370
  65.3 15.9 %collective-permute-start.9 = (f32[2,8,1024]{2,1,0:T(8,128)S(1)}, f32[2,8,1024]{2,1,0:T(8,128)S(1)}, u32[]{:S(2)}, u32[]{:S(2)}) collective-permute-start(f32[2,8,1024]{2,1,0:T(8,128)S(1)} %get-tuple-element.23.own), channel_id=1, source_target_pairs={{4,8},{5,9},{6,10},{7,11},{8,4},{9,5},{10,6},{11,7},{12,16},{13,17... | collective-permute-start | bytes 196616 | tf_op jit(solution)/shard_map/ppermute | solution.py:370
  69.1 12.1 %collective-permute-start.8 = (f32[2,8,1024]{2,1,0:T(8,128)S(1)}, f32[2,8,1024]{2,1,0:T(8,128)S(1)}, u32[]{:S(2)}, u32[]{:S(2)}) collective-permute-start(f32[2,8,1024]{2,1,0:T(8,128)S(1)} %get-tuple-element.23.own), channel_id=1, source_target_pairs={{0,2},{1,3},{2,0},{3,1},{4,6},{5,7},{6,4},{7,5},{8,10},{9,11},{10,... | collective-permute-start | bytes 196616 | tf_op jit(solution)/shard_map/ppermute | solution.py:370
  71.8 13.7 %collective-permute-start.7 = (f32[2,8,1024]{2,1,0:T(8,128)S(1)}, f32[2,8,1024]{2,1,0:T(8,128)S(1)}, u32[]{:S(2)}, u32[]{:S(2)}) collective-permute-start(f32[2,8,1024]{2,1,0:T(8,128)S(1)} %get-tuple-element.23.own), channel_id=1, source_target_pairs={{2,4},{3,5},{4,2},{5,3},{6,8},{7,9},{8,6},{9,7},{10,12},{11,13},{1... | collective-permute-start | bytes 196616 | tf_op jit(solution)/shard_map/ppermute | solution.py:370
  85.4 8.0 %collective-permute-start.12 = (f32[8,8,1024]{2,1,0:T(8,128)S(1)}, f32[8,8,1024]{2,1,0:T(8,128)S(1)}, u32[]{:S(2)}, u32[]{:S(2)}) collective-permute-start(f32[8,8,1024]{2,1,0:T(8,128)S(1)} %pad_maximum_fusion.1), channel_id=1, source_target_pairs={{0,1},{1,0},{2,3},{3,2},{4,5},{5,4},{6,7},{7,6},{8,9},{9,8},{10,11... | collective-permute-start | bytes 786440 | tf_op jit(solution)/shard_map/ppermute | solution.py:370
  88.3 20.6 %collective-permute-start.17 = (f32[3,8,2048]{2,1,0:T(8,128)S(1)}, f32[3,8,2048]{2,1,0:T(8,128)S(1)}, u32[]{:S(2)}, u32[]{:S(2)}) collective-permute-start(f32[3,8,2048]{2,1,0:T(8,128)S(1)} %get-tuple-element.32), channel_id=1, source_target_pairs={{0,8},{1,73},{2,10},{3,75},{4,12},{5,77},{6,14},{7,79},{8,64},{9,1... | collective-permute-start | bytes 589832 | tf_op jit(solution)/shard_map/ppermute | solution.py:392
  90.2 3.1 %collective-permute-start.6 = (f32[2,8,1024]{2,1,0:T(8,128)S(1)}, f32[2,8,1024]{2,1,0:T(8,128)S(1)}, u32[]{:S(2)}, u32[]{:S(2)}) collective-permute-start(f32[2,8,1024]{2,1,0:T(8,128)S(1)} %get-tuple-element.23.own), channel_id=1, source_target_pairs={{0,1},{1,0},{2,3},{3,2},{4,5},{5,4},{6,7},{7,6},{8,9},{9,8},{10,11... | collective-permute-start | bytes 196616 | tf_op jit(solution)/shard_map/ppermute | solution.py:370
  102.8 19.4 %collective-permute-start.13 = (f32[3,8,1024]{2,1,0:T(8,128)S(1)}, f32[3,8,1024]{2,1,0:T(8,128)S(1)}, u32[]{:S(2)}, u32[]{:S(2)}) collective-permute-start(f32[3,8,1024]{2,1,0:T(8,128)S(1)} %get-tuple-element.29), channel_id=1, source_target_pairs={{0,128},{64,192},{128,256},{192,320},{256,384},{320,448},{1,129},{... | collective-permute-start | bytes 294920 | tf_op jit(solution)/shard_map/ppermute | solution.py:375
  106.3 15.9 %collective-permute-start.14 = (f32[3,8,1024]{2,1,0:T(8,128)S(1)}, f32[3,8,1024]{2,1,0:T(8,128)S(1)}, u32[]{:S(2)}, u32[]{:S(2)}) collective-permute-start(f32[3,8,1024]{2,1,0:T(8,128)S(1)} %get-tuple-element.30), channel_id=1, source_target_pairs={{0,256},{64,320},{128,384},{192,448},{1,257},{65,321},{129,385},{1... | collective-permute-start | bytes 294920 | tf_op jit(solution)/shard_map/ppermute | solution.py:375
  108.3 13.9 %collective-permute-start.15 = (f32[3,8,1024]{2,1,0:T(8,128)S(1)}, f32[3,8,1024]{2,1,0:T(8,128)S(1)}, u32[]{:S(2)}, u32[]{:S(2)}) collective-permute-start(f32[3,8,1024]{2,1,0:T(8,128)S(1)} %get-tuple-element.31), channel_id=1, source_target_pairs={{0,384},{64,448},{1,385},{65,449},{2,386},{66,450},{3,387},{67,451... | collective-permute-start | bytes 294920 | tf_op jit(solution)/shard_map/ppermute | solution.py:375
  109.0 23.7 %collective-permute-start.18 = (f32[3,8,2048]{2,1,0:T(8,128)S(1)}, f32[3,8,2048]{2,1,0:T(8,128)S(1)}, u32[]{:S(2)}, u32[]{:S(2)}) collective-permute-start(f32[3,8,2048]{2,1,0:T(8,128)S(1)} %collective-permute-done.17), channel_id=1, source_target_pairs={{8,64},{73,65},{10,66},{75,67},{12,68},{77,69},{14,70},{79,71},{64... | collective-permute-start | bytes 589832 | tf_op jit(solution)/shard_map/ppermute | solution.py:392
  122.3 18.5 %collective-permute-start.16 = (f32[2,8,1024]{2,1,0:T(8,128)S(1)}, f32[2,8,1024]{2,1,0:T(8,128)S(1)}, u32[]{:S(2)}, u32[]{:S(2)}) collective-permute-start(f32[2,8,1024]{2,1,0:T(8,128)S(1)} %slice.4), channel_id=1, source_target_pairs={{0,64},{64,128},{128,192},{192,256},{256,320},{320,384},{384,448},... | collective-permute-start | bytes 196616 | tf_op jit(solution)/shard_map/ppermute | solution.py:375

commit v2 on v1

--- a/solution.py
+++ b/solution.py
@@ -13,7 +13,7 @@
 TIME_STEP = 0.28
 ROWS = 8
 LANES = 128
-GROUP = 8
+GROUP = 16
 
 ALPHA = 0.6265382932707997
 QUAD_A = 0.3734617067292003
@@ -324,7 +324,7 @@
             reach = -(-2 * (18 - 3 * s - n - 1) // ROWS)
             return range(5 - reach, 6 + reach)
 
-        coarse_step((one, two, three), window, tiles_of, half, 4)
+        coarse_step((one, two, three), window, tiles_of, half, 8)
         out = outs[s // 2]
         for k in range(half):
             lanes = pl.ds(k * LANES, LANES)
@@ -375,7 +375,7 @@
     return lax.ppermute(block, "tm", [(m, m + distance) for m in range(slices - distance)])
 
 
-def in_two_legs(block):
+def two_legs():
     slices, count = lax.axis_size("tm"), lax.axis_size("space")
     run = min(8, count // 2)
     legs = [], []
@@ -388,9 +388,7 @@
             stop = (2 * y + upper) * count + 2 * (group * run + low) + i % 2
             legs[0].append((m * count + i, stop))
             legs[1].append((stop, (m + 1) * count + i))
-    for leg in legs:
-        block = lax.ppermute(block, ("tm", "space"), leg)
-    return block
+    return legs
 
 
 def sibling(i):
@@ -453,14 +451,16 @@
         "fine",
         pos, state, vertical_field, a, b, q, sib, sib_a, sib_b, short,
     )
-    arrived = in_two_legs(detail)
+    legs = two_legs()
+    halfway = lax.ppermute(detail, ("tm", "space"), legs[0])
     sib = swap(message, sibling)
     b = swap(message, near_even)
     d = swap(message, far_even)
     q = swap(message, fifth)
     c = swap(message, far_odd)
     a = swap(message, near_odd)
-    a, b, c, d, q = lax.optimization_barrier((a, b, c, d, q))
+    a, b, c, d, q, sib, halfway = lax.optimization_barrier((a, b, c, d, q, sib, halfway))
+    arrived = lax.ppermute(halfway, ("tm", "space"), legs[1])
     others = swap(jnp.concatenate([a, b, c, d], axis=0), sibling)
     powers = call(
         functools.partial(powers_kernel, count, strips),
@@ -469,6 +469,7 @@
         "powers",
         pos, message, sib, a, b, c, d, q, others,
     )
+    powers, arrived = lax.optimization_barrier((powers, arrived))
     own = sum(later(x, 2 * d + 2) for d, x in enumerate(powers))
     other = later(own[1:], 1)
     (new_start,) = call(

time: 143 us -> 141 us (0.986)
  the two profiles are of different devices: /device:TPU:10 before, /device:TPU:28 now
where the time goes in v2:
time: 141 us; the launch traced here: 140 us
  starting transfers between devices  74.7 us (53%)
  waiting for transfers between devices  40.6 us (29%)
  Pallas kernels  22.8 us (16%)
    ppermute x13, starting transfers between devices, swap(): return lax.ppermute(block, 'space', pairs)  56.4 us
    pallas_call x4, Pallas kernels, call(): pl.pallas_call(kernel, out_shape=outs, in_specs=[SMEM] + [VMEM] * (len(ar...  22.8 us
    ppermute x4, waiting for transfers between devices, later(): lax.ppermute(block, 'tm', [(m, m + distance) for m in range(slices - dist...  19.4 us
    ppermute x13, waiting for transfers between devices, swap(): return lax.ppermute(block, 'space', pairs)  16 us
    ppermute x4, starting transfers between devices, later(): lax.ppermute(block, 'tm', [(m, m + distance) for m in range(slices - dist...  8.73 us
    ppermute x1, starting transfers between devices, body(): halfway = lax.ppermute(detail, ('tm', 'space'), legs[0])  8.33 us
    ppermute x1, waiting for transfers between devices, body(): arrived = lax.ppermute(halfway, ('tm', 'space'), legs[1])  5.11 us
  transfers between devices with their start and end apart: 19, of which 9 were waited for; matrix products, arithmetic and copies ran while one was open for 0% of the time, Pallas kernels for 5%

profile of v2, /device:TPU:28, one launch (start us, length us, event | category | flops | bytes accessed | tf_op | source)
XLA Modules:
  0.0 140.1 jit_solution(15432418108204288349)
XLA Ops:
  1.7 11.2 %collective-permute-start.2 = (f32[4,8,2048]{2,1,0:T(8,128)S(1)}, f32[4,8,2048]{2,1,0:T(8,128)S(1)}, u32[]{:S(2)}, u32[]{:S(2)}) collective-permute-start(f32[4,8,2048]{2,1,0:T(8,128)S(1)} %pad_maximum_fusion), channel_id=1, source_target_pairs={{1,4},{3,6},{4,1},{5,8},{6,3},{7,10},{8,5},{9,12},{10,7},{11,14},{... | collective-permute-start | bytes 786440 | tf_op jit(solution)/shard_map/ppermute | solution.py:370
  12.9 3.8 %collective-permute-start.1 = (f32[4,8,2048]{2,1,0:T(8,128)S(1)}, f32[4,8,2048]{2,1,0:T(8,128)S(1)}, u32[]{:S(2)}, u32[]{:S(2)}) collective-permute-start(f32[4,8,2048]{2,1,0:T(8,128)S(1)} %pad_maximum_fusion), channel_id=1, source_target_pairs={{0,2},{1,3},{2,0},{3,1},{4,6},{5,7},{6,4},{7,5},{8,10},{9,11},{10,... | collective-permute-start | bytes 786440 | tf_op jit(solution)/shard_map/ppermute | solution.py:370
  16.7 2.0 %collective-permute-start = (f32[4,8,2048]{2,1,0:T(8,128)S(1)}, f32[4,8,2048]{2,1,0:T(8,128)S(1)}, u32[]{:S(2)}, u32[]{:S(2)}) collective-permute-start(f32[4,8,2048]{2,1,0:T(8,128)S(1)} %pad_maximum_fusion), channel_id=1, source_target_pairs={{2,4},{3,5},{4,2},{5,3},{6,8},{7,9},{8,6},{9,7},{10,12},{11,13},{1... | collective-permute-start | bytes 786440 | tf_op jit(solution)/shard_map/ppermute | solution.py:370
  20.7 3.9 %collective-permute-done.2.third = f32[4,8,2048]{2,1,0:T(8,128)S(1)} collective-permute-done((f32[4,8,2048]{2,1,0:T(8,128)S(1)}, f32[4,8,2048]{2,1,0:T(8,128)S(1)}, u32[]{:S(2)}, u32[]{:S(2)}) %collective-permute-start.2) | collective-permute-done | bytes 262176 | tf_op jit(solution)/shard_map/ppermute | solution.py:370
  24.6 8.0 %collective-permute-done.near_a = f32[4,8,2048]{2,1,0:T(8,128)S(1)} collective-permute-done((f32[4,8,2048]{2,1,0:T(8,128)S(1)}, f32[4,8,2048]{2,1,0:T(8,128)S(1)}, u32[]{:S(2)}, u32[]{:S(2)}) %collective-permute-start) | collective-permute-done | bytes 262176 | tf_op jit(solution)/shard_map/ppermute | solution.py:370
  34.6 2.4 %collective-permute-start.5 = (f32[4,8,2048]{2,1,0:T(8,128)S(1)}, f32[4,8,2048]{2,1,0:T(8,128)S(1)}, u32[]{:S(2)}, u32[]{:S(2)}) collective-permute-start(f32[4,8,2048]{2,1,0:T(8,128)S(1)} %collective-permute-done.1.near_b), channel_id=1, source_target_pairs={{0,1},{1,0},{2,3},{3,2},{4,5},{5,4},{6,7},{7,6},{8,9},{9,8},{10,11... | collective-permute-start | bytes 786440 | tf_op jit(solution)/shard_map/ppermute | solution.py:370
  38.1 2.4 %coarse.1 = (f32[3,8,2048]{2,1,0:T(8,128)}, f32[3,8,1024]{2,1,0:T(8,128)S(1)}) custom-call(s32[2]{0:T(128)S(1)} %pad_add_fusion.pos, f32[3,8,2048]{2,1,0:T(8,128)S(1)} %bitcast.8, f32[8,2048]{1,0:T(8,128)S(1)} %copy-done.1, f32[4,8,2048]{2,1,0:T(8,128)S(1)} %collective-permute-done.3.sib, f32[4,8,2048]{2,1,0:T(8,128)S(1)} %collective-permute-done.4.sib_a, ...), custom_call_target="tpu_custom_call" | custom-call | tf_op jit(solution)/shard_map/coarse/pallas_call | solution.py:355
  40.6 12.0 %fine.1 = (f32[3,8,2048]{2,1,0:T(8,128)}, f32[3,8,2048]{2,1,0:T(8,128)S(1)}, f32[2,8,1024]{2,1,0:T(8,128)S(1)}) custom-call(s32[2]{0:T(128)S(1)} %pad_add_fusion.pos, f32[3,8,2048]{2,1,0:T(8,128)S(1)} %bitcast.9, f32[8,2048]{1,0:T(8,128)S(1)} %copy-done.1, f32[4,8,2048]{2,1,0:T(8,128)S(1)} %collective-permute-done.near_a, ...), custom_call_target="tpu_custom_call" | custom-call | tf_op jit(solution)/shard_map/fine/pallas_call | solution.py:355
  52.5 8.3 %collective-permute-start.12 = (f32[3,8,2048]{2,1,0:T(8,128)S(1)}, f32[3,8,2048]{2,1,0:T(8,128)S(1)}, u32[]{:S(2)}, u32[]{:S(2)}) collective-permute-start(f32[3,8,2048]{2,1,0:T(8,128)S(1)} %get-tuple-element.30), channel_id=1, source_target_pairs={{0,8},{1,73},{2,10},{3,75},{4,12},{5,77},{6,14},{7,79},{8,64},{9,1... | collective-permute-start | bytes 589832 | tf_op jit(solution)/shard_map/ppermute | solution.py:455
  60.9 3.9 %collective-permute-start.11 = (f32[2,8,1024]{2,1,0:T(8,128)S(1)}, f32[2,8,1024]{2,1,0:T(8,128)S(1)}, u32[]{:S(2)}, u32[]{:S(2)}) collective-permute-start(f32[2,8,1024]{2,1,0:T(8,128)S(1)} %get-tuple-element.29.own), channel_id=1, source_target_pairs={{0,1},{1,0},{2,3},{3,2},{4,5},{5,4},{6,7},{7,6},{8,9},{9,8},{10,11... | collective-permute-start | bytes 196616 | tf_op jit(solution)/shard_map/ppermute | solution.py:370
  64.8 5.2 %collective-permute-start.10 = (f32[2,8,1024]{2,1,0:T(8,128)S(1)}, f32[2,8,1024]{2,1,0:T(8,128)S(1)}, u32[]{:S(2)}, u32[]{:S(2)}) collective-permute-start(f32[2,8,1024]{2,1,0:T(8,128)S(1)} %get-tuple-element.29.own), channel_id=1, source_target_pairs={{1,6},{3,8},{5,10},{6,1},{7,12},{8,3},{9,14},{10,5},{11,16},{12,7}... | collective-permute-start | bytes 196616 | tf_op jit(solution)/shard_map/ppermute | solution.py:370
  70.0 4.6 %collective-permute-start.9 = (f32[2,8,1024]{2,1,0:T(8,128)S(1)}, f32[2,8,1024]{2,1,0:T(8,128)S(1)}, u32[]{:S(2)}, u32[]{:S(2)}) collective-permute-start(f32[2,8,1024]{2,1,0:T(8,128)S(1)} %get-tuple-element.29.own), channel_id=1, source_target_pairs={{0,4},{1,5},{2,6},{3,7},{4,0},{5,1},{6,2},{7,3},{8,12},{9,13},{10,... | collective-permute-start | bytes 196616 | tf_op jit(solution)/shard_map/ppermute | solution.py:370
  74.6 2.7 %collective-permute-start.8 = (f32[2,8,1024]{2,1,0:T(8,128)S(1)}, f32[2,8,1024]{2,1,0:T(8,128)S(1)}, u32[]{:S(2)}, u32[]{:S(2)}) collective-permute-start(f32[2,8,1024]{2,1,0:T(8,128)S(1)} %get-tuple-element.29.own), channel_id=1, source_target_pairs={{4,8},{5,9},{6,10},{7,11},{8,4},{9,5},{10,6},{11,7},{12,16},{13,17... | collective-permute-start | bytes 196616 | tf_op jit(solution)/shard_map/ppermute | solution.py:370
  77.3 2.4 %collective-permute-start.7 = (f32[2,8,1024]{2,1,0:T(8,128)S(1)}, f32[2,8,1024]{2,1,0:T(8,128)S(1)}, u32[]{:S(2)}, u32[]{:S(2)}) collective-permute-start(f32[2,8,1024]{2,1,0:T(8,128)S(1)} %get-tuple-element.29.own), channel_id=1, source_target_pairs={{0,2},{1,3},{2,0},{3,1},{4,6},{5,7},{6,4},{7,5},{8,10},{9,11},{10,... | collective-permute-start | bytes 196616 | tf_op jit(solution)/shard_map/ppermute | solution.py:370
  79.8 10.7 %collective-permute-start.6 = (f32[2,8,1024]{2,1,0:T(8,128)S(1)}, f32[2,8,1024]{2,1,0:T(8,128)S(1)}, u32[]{:S(2)}, u32[]{:S(2)}) collective-permute-start(f32[2,8,1024]{2,1,0:T(8,128)S(1)} %get-tuple-element.29.own), channel_id=1, source_target_pairs={{2,4},{3,5},{4,2},{5,3},{6,8},{7,9},{8,6},{9,7},{10,12},{11,13},{1... | collective-permute-start | bytes 196616 | tf_op jit(solution)/shard_map/ppermute | solution.py:370
  90.5 3.0 %collective-permute-done.6.near_a = f32[2,8,1024]{2,1,0:T(8,128)S(1)} collective-permute-done((f32[2,8,1024]{2,1,0:T(8,128)S(1)}, f32[2,8,1024]{2,1,0:T(8,128)S(1)}, u32[]{:S(2)}, u32[]{:S(2)}) %collective-permute-start.6) | collective-permute-done | bytes 65568 | tf_op jit(solution)/shard_map/ppermute | solution.py:370
  93.5 3.5 %collective-permute-start.13 = (f32[8,8,1024]{2,1,0:T(8,128)S(1)}, f32[8,8,1024]{2,1,0:T(8,128)S(1)}, u32[]{:S(2)}, u32[]{:S(2)}) collective-permute-start(f32[8,8,1024]{2,1,0:T(8,128)S(1)} %pad_maximum_fusion.1), channel_id=1, source_target_pairs={{0,1},{1,0},{2,3},{3,2},{4,5},{5,4},{6,7},{7,6},{8,9},{9,8},{10,11... | collective-permute-start | bytes 786440 | tf_op jit(solution)/shard_map/ppermute | solution.py:370
  98.4 7.1 %powers.1 = (f32[3,8,1024]{2,1,0:T(8,128)S(1)}, f32[3,8,1024]{2,1,0:T(8,128)S(1)}, f32[3,8,1024]{2,1,0:T(8,128)S(1)}) custom-call(s32[2]{0:T(128)S(1)} %pad_add_fusion.pos, f32[2,8,1024]{2,1,0:T(8,128)S(1)} %get-tuple-element.29.own, f32[2,8,1024]{2,1,0:T(8,128)S(1)} %collective-permute-done.11.sib, f32[2,8,1024]{2,1,0:T(8,128)S(1)} %collective-permute-done.6.near_a, ...), custom_call_target="tpu_custom_call" | custom-call | tf_op jit(solution)/shard_map/powers/pallas_call | solution.py:355
  105.5 5.1 %collective-permute-done.14.detail = f32[3,8,2048]{2,1,0:T(8,128)S(1)} collective-permute-done((f32[3,8,2048]{2,1,0:T(8,128)S(1)}, f32[3,8,2048]{2,1,0:T(8,128)S(1)}, u32[]{:S(2)}, u32[]{:S(2)}) %collective-permute-start.14) | collective-permute-done | bytes 196640 | tf_op jit(solution)/shard_map/ppermute | solution.py:463
  114.5 2.6 %collective-permute-done.15 = f32[3,8,1024]{2,1,0:T(8,128)S(1)} collective-permute-done((f32[3,8,1024]{2,1,0:T(8,128)S(1)}, f32[3,8,1024]{2,1,0:T(8,128)S(1)}, u32[]{:S(2)}, u32[]{:S(2)}) %collective-permute-start.15) | collective-permute-done | bytes 98336 | tf_op jit(solution)/shard_map/ppermute | solution.py:375
  117.1 2.8 %collective-permute-done.16 = f32[3,8,1024]{2,1,0:T(8,128)S(1)} collective-permute-done((f32[3,8,1024]{2,1,0:T(8,128)S(1)}, f32[3,8,1024]{2,1,0:T(8,128)S(1)}, u32[]{:S(2)}, u32[]{:S(2)}) %collective-permute-start.16) | collective-permute-done | bytes 98336 | tf_op jit(solution)/shard_map/ppermute | solution.py:375
  119.9 3.1 %collective-permute-done.17 = f32[3,8,1024]{2,1,0:T(8,128)S(1)} collective-permute-done((f32[3,8,1024]{2,1,0:T(8,128)S(1)}, f32[3,8,1024]{2,1,0:T(8,128)S(1)}, u32[]{:S(2)}, u32[]{:S(2)}) %collective-permute-start.17) | collective-permute-done | bytes 98336 | tf_op jit(solution)/shard_map/ppermute | solution.py:375
  123.0 4.9 %collective-permute-start.18 = (f32[2,8,1024]{2,1,0:T(8,128)S(1)}, f32[2,8,1024]{2,1,0:T(8,128)S(1)}, u32[]{:S(2)}, u32[]{:S(2)}) collective-permute-start(f32[2,8,1024]{2,1,0:T(8,128)S(1)} %slice.4), channel_id=1, source_target_pairs={{0,64},{64,128},{128,192},{192,256},{256,320},{320,384},{384,448},... | collective-permute-start | bytes 196616 | tf_op jit(solution)/shard_map/ppermute | solution.py:375
  127.9 10.9 %collective-permute-done.18.other = f32[2,8,1024]{2,1,0:T(8,128)S(1)} collective-permute-done((f32[2,8,1024]{2,1,0:T(8,128)S(1)}, f32[2,8,1024]{2,1,0:T(8,128)S(1)}, u32[]{:S(2)}, u32[]{:S(2)}) %collective-permute-start.18) | collective-permute-done | bytes 65568 | tf_op jit(solution)/shard_map/ppermute | solution.py:375
  (27 shorter events, 12.6 us)
Async XLA Ops:
  0.6 37.5 %copy-start = (f32[1,3,8,2048]{3,2,1,0:T(8,128)S(1)}, f32[1,3,8,2048]{3,2,1,0:T(8,128)}, u32[]{:S(2)}) copy-start(f32[1,3,8,2048]{3,2,1,0:T(8,128)} %param.2) | copy-start | bytes 589828
  0.6 37.5 %copy-start.1 = (f32[8,2048]{1,0:T(8,128)S(1)}, f32[8,2048]{1,0:T(8,128)}, u32[]{:S(2)}) copy-start(f32[8,2048]{1,0:T(8,128)} %field.3) | copy-start | bytes 196612
  1.7 23.0 %collective-permute-start.2 = (f32[4,8,2048]{2,1,0:T(8,128)S(1)}, f32[4,8,2048]{2,1,0:T(8,128)S(1)}, u32[]{:S(2)}, u32[]{:S(2)}) collective-permute-start(f32[4,8,2048]{2,1,0:T(8,128)S(1)} %pad_maximum_fusion), channel_id=1, source_target_pairs={{1,4},{3,6},{4,1},{5,8},{6,3},{7,10},{8,5},{9,12},{10,7},{11,14},{... | collective-permute-start | bytes 786440 | tf_op jit(solution)/shard_map/ppermute | solution.py:370
  12.9 11.7 %collective-permute-start.1 = (f32[4,8,2048]{2,1,0:T(8,128)S(1)}, f32[4,8,2048]{2,1,0:T(8,128)S(1)}, u32[]{:S(2)}, u32[]{:S(2)}) collective-permute-start(f32[4,8,2048]{2,1,0:T(8,128)S(1)} %pad_maximum_fusion), channel_id=1, source_target_pairs={{0,2},{1,3},{2,0},{3,1},{4,6},{5,7},{6,4},{7,5},{8,10},{9,11},{10,... | collective-permute-start | bytes 786440 | tf_op jit(solution)/shard_map/ppermute | solution.py:370
  16.7 15.9 %collective-permute-start = (f32[4,8,2048]{2,1,0:T(8,128)S(1)}, f32[4,8,2048]{2,1,0:T(8,128)S(1)}, u32[]{:S(2)}, u32[]{:S(2)}) collective-permute-start(f32[4,8,2048]{2,1,0:T(8,128)S(1)} %pad_maximum_fusion), channel_id=1, source_target_pairs={{2,4},{3,5},{4,2},{5,3},{6,8},{7,9},{8,6},{9,7},{10,12},{11,13},{1... | collective-permute-start | bytes 786440 | tf_op jit(solution)/shard_map/ppermute | solution.py:370
  18.8 18.3 %collective-permute-start.3 = (f32[4,8,2048]{2,1,0:T(8,128)S(1)}, f32[4,8,2048]{2,1,0:T(8,128)S(1)}, u32[]{:S(2)}, u32[]{:S(2)}) collective-permute-start(f32[4,8,2048]{2,1,0:T(8,128)S(1)} %pad_maximum_fusion), channel_id=1, source_target_pairs={{0,1},{1,0},{2,3},{3,2},{4,5},{5,4},{6,7},{7,6},{8,9},{9,8},{10,11... | collective-permute-start | bytes 786440 | tf_op jit(solution)/shard_map/ppermute | solution.py:370
  32.7 4.4 %collective-permute-start.4 = (f32[4,8,2048]{2,1,0:T(8,128)S(1)}, f32[4,8,2048]{2,1,0:T(8,128)S(1)}, u32[]{:S(2)}, u32[]{:S(2)}) collective-permute-start(f32[4,8,2048]{2,1,0:T(8,128)S(1)} %collective-permute-done.near_a), channel_id=1, source_target_pairs={{0,1},{1,0},{2,3},{3,2},{4,5},{5,4},{6,7},{7,6},{8,9},{9,8},{10,11... | collective-permute-start | bytes 786440 | tf_op jit(solution)/shard_map/ppermute | solution.py:370
  34.6 3.6 %collective-permute-start.5 = (f32[4,8,2048]{2,1,0:T(8,128)S(1)}, f32[4,8,2048]{2,1,0:T(8,128)S(1)}, u32[]{:S(2)}, u32[]{:S(2)}) collective-permute-start(f32[4,8,2048]{2,1,0:T(8,128)S(1)} %collective-permute-done.1.near_b), channel_id=1, source_target_pairs={{0,1},{1,0},{2,3},{3,2},{4,5},{5,4},{6,7},{7,6},{8,9},{9,8},{10,11... | collective-permute-start | bytes 786440 | tf_op jit(solution)/shard_map/ppermute | solution.py:370
  52.5 41.0 %collective-permute-start.12 = (f32[3,8,2048]{2,1,0:T(8,128)S(1)}, f32[3,8,2048]{2,1,0:T(8,128)S(1)}, u32[]{:S(2)}, u32[]{:S(2)}) collective-permute-start(f32[3,8,2048]{2,1,0:T(8,128)S(1)} %get-tuple-element.30), channel_id=1, source_target_pairs={{0,8},{1,73},{2,10},{3,75},{4,12},{5,77},{6,14},{7,79},{8,64},{9,1... | collective-permute-start | bytes 589832 | tf_op jit(solution)/shard_map/ppermute | solution.py:455
  60.9 16.5 %collective-permute-start.11 = (f32[2,8,1024]{2,1,0:T(8,128)S(1)}, f32[2,8,1024]{2,1,0:T(8,128)S(1)}, u32[]{:S(2)}, u32[]{:S(2)}) collective-permute-start(f32[2,8,1024]{2,1,0:T(8,128)S(1)} %get-tuple-element.29.own), channel_id=1, source_target_pairs={{0,1},{1,0},{2,3},{3,2},{4,5},{5,4},{6,7},{7,6},{8,9},{9,8},{10,11... | collective-permute-start | bytes 196616 | tf_op jit(solution)/shard_map/ppermute | solution.py:370
  64.8 15.0 %collective-permute-start.10 = (f32[2,8,1024]{2,1,0:T(8,128)S(1)}, f32[2,8,1024]{2,1,0:T(8,128)S(1)}, u32[]{:S(2)}, u32[]{:S(2)}) collective-permute-start(f32[2,8,1024]{2,1,0:T(8,128)S(1)} %get-tuple-element.29.own), channel_id=1, source_target_pairs={{1,6},{3,8},{5,10},{6,1},{7,12},{8,3},{9,14},{10,5},{11,16},{12,7}... | collective-permute-start | bytes 196616 | tf_op jit(solution)/shard_map/ppermute | solution.py:370
  70.0 20.5 %collective-permute-start.9 = (f32[2,8,1024]{2,1,0:T(8,128)S(1)}, f32[2,8,1024]{2,1,0:T(8,128)S(1)}, u32[]{:S(2)}, u32[]{:S(2)}) collective-permute-start(f32[2,8,1024]{2,1,0:T(8,128)S(1)} %get-tuple-element.29.own), channel_id=1, source_target_pairs={{0,4},{1,5},{2,6},{3,7},{4,0},{5,1},{6,2},{7,3},{8,12},{9,13},{10,... | collective-permute-start | bytes 196616 | tf_op jit(solution)/shard_map/ppermute | solution.py:370
  74.6 15.9 %collective-permute-start.8 = (f32[2,8,1024]{2,1,0:T(8,128)S(1)}, f32[2,8,1024]{2,1,0:T(8,128)S(1)}, u32[]{:S(2)}, u32[]{:S(2)}) collective-permute-start(f32[2,8,1024]{2,1,0:T(8,128)S(1)} %get-tuple-element.29.own), channel_id=1, source_target_pairs={{4,8},{5,9},{6,10},{7,11},{8,4},{9,5},{10,6},{11,7},{12,16},{13,17... | collective-permute-start | bytes 196616 | tf_op jit(solution)/shard_map/ppermute | solution.py:370
  77.3 13.2 %collective-permute-start.7 = (f32[2,8,1024]{2,1,0:T(8,128)S(1)}, f32[2,8,1024]{2,1,0:T(8,128)S(1)}, u32[]{:S(2)}, u32[]{:S(2)}) collective-permute-start(f32[2,8,1024]{2,1,0:T(8,128)S(1)} %get-tuple-element.29.own), channel_id=1, source_target_pairs={{0,2},{1,3},{2,0},{3,1},{4,6},{5,7},{6,4},{7,5},{8,10},{9,11},{10,... | collective-permute-start | bytes 196616 | tf_op jit(solution)/shard_map/ppermute | solution.py:370
  79.8 13.7 %collective-permute-start.6 = (f32[2,8,1024]{2,1,0:T(8,128)S(1)}, f32[2,8,1024]{2,1,0:T(8,128)S(1)}, u32[]{:S(2)}, u32[]{:S(2)}) collective-permute-start(f32[2,8,1024]{2,1,0:T(8,128)S(1)} %get-tuple-element.29.own), channel_id=1, source_target_pairs={{2,4},{3,5},{4,2},{5,3},{6,8},{7,9},{8,6},{9,7},{10,12},{11,13},{1... | collective-permute-start | bytes 196616 | tf_op jit(solution)/shard_map/ppermute | solution.py:370
  93.5 4.8 %collective-permute-start.13 = (f32[8,8,1024]{2,1,0:T(8,128)S(1)}, f32[8,8,1024]{2,1,0:T(8,128)S(1)}, u32[]{:S(2)}, u32[]{:S(2)}) collective-permute-start(f32[8,8,1024]{2,1,0:T(8,128)S(1)} %pad_maximum_fusion.1), channel_id=1, source_target_pairs={{0,1},{1,0},{2,3},{3,2},{4,5},{5,4},{6,7},{7,6},{8,9},{9,8},{10,11... | collective-permute-start | bytes 786440 | tf_op jit(solution)/shard_map/ppermute | solution.py:370
  97.1 13.5 %collective-permute-start.14 = (f32[3,8,2048]{2,1,0:T(8,128)S(1)}, f32[3,8,2048]{2,1,0:T(8,128)S(1)}, u32[]{:S(2)}, u32[]{:S(2)}) collective-permute-start(f32[3,8,2048]{2,1,0:T(8,128)S(1)} %collective-permute-done.12), channel_id=1, source_target_pairs={{8,64},{73,65},{10,66},{75,67},{12,68},{77,69},{14,70},{79,71},{64... | collective-permute-start | bytes 589832 | tf_op jit(solution)/shard_map/ppermute | solution.py:463
  110.6 6.5 %collective-permute-start.15 = (f32[3,8,1024]{2,1,0:T(8,128)S(1)}, f32[3,8,1024]{2,1,0:T(8,128)S(1)}, u32[]{:S(2)}, u32[]{:S(2)}) collective-permute-start(f32[3,8,1024]{2,1,0:T(8,128)S(1)} %get-tuple-element.41), channel_id=1, source_target_pairs={{0,128},{64,192},{128,256},{192,320},{256,384},{320,448},{1,129},{... | collective-permute-start | bytes 294920 | tf_op jit(solution)/shard_map/ppermute | solution.py:375
  111.9 8.0 %collective-permute-start.16 = (f32[3,8,1024]{2,1,0:T(8,128)S(1)}, f32[3,8,1024]{2,1,0:T(8,128)S(1)}, u32[]{:S(2)}, u32[]{:S(2)}) collective-permute-start(f32[3,8,1024]{2,1,0:T(8,128)S(1)} %get-tuple-element.42), channel_id=1, source_target_pairs={{0,256},{64,320},{128,384},{192,448},{1,257},{65,321},{129,385},{1... | collective-permute-start | bytes 294920 | tf_op jit(solution)/shard_map/ppermute | solution.py:375
  113.2 9.8 %collective-permute-start.17 = (f32[3,8,1024]{2,1,0:T(8,128)S(1)}, f32[3,8,1024]{2,1,0:T(8,128)S(1)}, u32[]{:S(2)}, u32[]{:S(2)}) collective-permute-start(f32[3,8,1024]{2,1,0:T(8,128)S(1)} %get-tuple-element.43), channel_id=1, source_target_pairs={{0,384},{64,448},{1,385},{65,449},{2,386},{66,450},{3,387},{67,451... | collective-permute-start | bytes 294920 | tf_op jit(solution)/shard_map/ppermute | solution.py:375
  123.0 15.8 %collective-permute-start.18 = (f32[2,8,1024]{2,1,0:T(8,128)S(1)}, f32[2,8,1024]{2,1,0:T(8,128)S(1)}, u32[]{:S(2)}, u32[]{:S(2)}) collective-permute-start(f32[2,8,1024]{2,1,0:T(8,128)S(1)} %slice.4), channel_id=1, source_target_pairs={{0,64},{64,128},{128,192},{192,256},{256,320},{320,384},{384,448},... | collective-permute-start | bytes 196616 | tf_op jit(solution)/shard_map/ppermute | solution.py:375

commit v3 on v2

--- a/solution.py
+++ b/solution.py
@@ -13,7 +13,6 @@
 TIME_STEP = 0.28
 ROWS = 8
 LANES = 128
-GROUP = 16
 
 ALPHA = 0.6265382932707997
 QUAD_A = 0.3734617067292003
@@ -32,6 +31,15 @@
 def strip(k):
     start = LANES + k * LANES
     return pl.ds(start if isinstance(start, int) else pl.multiple_of(start, LANES), LANES)
+
+
+def guard_pair(sign, first, last, shift, even):
+    low = sign * pltpu.roll(first, LANES - shift, 1)
+    high = sign * pltpu.roll(last, shift, 1)
+    if shift == 2:
+        low = jnp.where(even, low, pltpu.roll(last, 1, 1))
+        high = jnp.where(even, pltpu.roll(first, LANES - 1, 1), high)
+    return low, high
 
 
 def guards(buf, tiles, shift, strips):
@@ -41,16 +49,12 @@
         for comp, sign in ((0, 1.0), (2, -1.0)):
             first = buf[t, comp, :, strip(0)]
             last = buf[t, comp, :, strip(strips - 1)]
-            low = sign * pltpu.roll(first, LANES - shift, 1)
-            high = sign * pltpu.roll(last, shift, 1)
-            if shift == 2:
-                low = jnp.where(even, low, pltpu.roll(last, 1, 1))
-                high = jnp.where(even, pltpu.roll(first, LANES - 1, 1), high)
+            low, high = guard_pair(sign, first, last, shift, even)
             buf[t, comp, :, strip(-1)] = low
             buf[t, comp, :, strip(strips)] = high
 
 
-def stage(dst, src, base, weight, length, field, tiles, shift, cell, strips, group):
+def stage(dst, src, base, weight, length, field, tiles, shift, cell, strips):
     factor = length / (2.0 * cell)
     drag = FRICTION * length
     sub, lane = iotas()
@@ -59,54 +63,57 @@
     lanes_high = lane >= LANES - shift
     lanes_low = lane < shift
     slots = dst.shape[0]
-    group = min(group, strips)
-
-    def block(g, carry):
-        for j in range(group):
-            k = g * group + j
-            here = strip(k)
-            cache = {}
-
-            def get(comp, t):
-                t = min(max(t, 0), slots - 1)
-                if (comp, t) not in cache:
-                    cache[comp, t] = src[t, comp, :, here]
-                return cache[comp, t]
-
-            for t in tiles:
-                height, east, north = get(0, t), get(1, t), get(2, t)
-
-                def row_diff(comp, centre):
-                    before = jnp.where(rows_high, get(comp, t - 1), centre)
-                    after = jnp.where(rows_low, get(comp, t + 1), centre)
-                    return pltpu.roll(after, ROWS - shift, 0) - pltpu.roll(before, shift, 0)
-
-                def col_diff(comp, centre):
-                    before = jnp.where(lanes_high, src[t, comp, :, strip(k - 1)], centre)
-                    after = jnp.where(lanes_low, src[t, comp, :, strip(k + 1)], centre)
-                    return pltpu.roll(after, LANES - shift, 1) - pltpu.roll(before, shift, 1)
-
-                b = field[t, :, pl.ds(here.start - LANES, LANES)]
-                dx, dy = row_diff(0, height), col_diff(0, height)
-                rise = row_diff(1, east) + col_diff(2, north)
-                if base is src:
-                    new_height = weight * height - factor * rise
-                    new_east = (weight - drag) * east + factor * (b * dy - dx)
-                    new_north = (weight - drag) * north - factor * (b * dx + dy)
-                else:
-                    old = [base[t, comp, :, here] for comp in range(3)]
-                    if weight != 1.0:
-                        old = [weight * o for o in old]
-                    new_height = old[0] - factor * rise
-                    new_east = old[1] - drag * east + factor * (b * dy - dx)
-                    new_north = old[2] - drag * north - factor * (b * dx + dy)
-                dst[t, 0, :, here] = new_height
-                dst[t, 1, :, here] = new_east
-                dst[t, 2, :, here] = new_north
-        return carry
-
-    lax.fori_loop(0, strips // group, block, 0)
-    guards(dst, tiles, shift, strips)
+    even = lane % 2 == 0
+    firsts = {}
+    for k in range(strips):
+        here = strip(k)
+        cache = {}
+
+        def get(comp, t):
+            t = min(max(t, 0), slots - 1)
+            if (comp, t) not in cache:
+                cache[comp, t] = src[t, comp, :, here]
+            return cache[comp, t]
+
+        for t in tiles:
+            height, east, north = get(0, t), get(1, t), get(2, t)
+
+            def row_diff(comp, centre):
+                before = jnp.where(rows_high, get(comp, t - 1), centre)
+                after = jnp.where(rows_low, get(comp, t + 1), centre)
+                return pltpu.roll(after, ROWS - shift, 0) - pltpu.roll(before, shift, 0)
+
+            def col_diff(comp, centre):
+                before = jnp.where(lanes_high, src[t, comp, :, strip(k - 1)], centre)
+                after = jnp.where(lanes_low, src[t, comp, :, strip(k + 1)], centre)
+                return pltpu.roll(after, LANES - shift, 1) - pltpu.roll(before, shift, 1)
+
+            b = field[t, :, pl.ds(here.start - LANES, LANES)]
+            dx, dy = row_diff(0, height), col_diff(0, height)
+            rise = row_diff(1, east) + col_diff(2, north)
+            if base is src:
+                new_height = weight * height - factor * rise
+                new_east = (weight - drag) * east + factor * (b * dy - dx)
+                new_north = (weight - drag) * north - factor * (b * dx + dy)
+            else:
+                old = [base[t, comp, :, here] for comp in range(3)]
+                if weight != 1.0:
+                    old = [weight * o for o in old]
+                new_height = old[0] - factor * rise
+                new_east = old[1] - drag * east + factor * (b * dy - dx)
+                new_north = old[2] - drag * north - factor * (b * dx + dy)
+            dst[t, 0, :, here] = new_height
+            dst[t, 1, :, here] = new_east
+            dst[t, 2, :, here] = new_north
+            if k == 0:
+                firsts[t] = new_height, new_north
+            if k == strips - 1:
+                for comp, sign, first, final in zip(
+                    (0, 2), (1.0, -1.0), firsts[t], (new_height, new_north)
+                ):
+                    low, high = guard_pair(sign, first, final, shift, even)
+                    dst[t, comp, :, strip(-1)] = low
+                    dst[t, comp, :, strip(strips)] = high
 
 
 def pair_mean(x, sub, lane):
@@ -207,7 +214,7 @@
     flip_state(one, position, count, 3)
     guards(one, range(7), 1, strips)
 
-    run = functools.partial(stage, field=window, shift=1, cell=1.0, strips=strips, group=GROUP)
+    run = functools.partial(stage, field=window, shift=1, cell=1.0, strips=strips)
     a, b = one, two
     for reach, quads, lines in ((3, 3, 2), (2, 3, 2), (1, 2, 4)):
         tiles = range(3 - reach, 4 + reach)
@@ -246,10 +253,10 @@
         message[1, :, lanes] = zipped(means[2], LORENTZ * folded(*sides, lane), sub)
 
 
-def coarse_step(bufs, field, tiles_of, strips, group):
+def coarse_step(bufs, field, tiles_of, strips):
     one, two, three = bufs
     length = FINE_STEPS * TIME_STEP
-    run = functools.partial(stage, base=one, field=field, shift=2, cell=2.0, strips=strips, group=group)
+    run = functools.partial(stage, base=one, field=field, shift=2, cell=2.0, strips=strips)
     run(two, one, weight=1.0, length=length / 3.0, tiles=tiles_of(0))
     run(three, two, weight=1.0, length=length / 2.0, tiles=tiles_of(1))
     run(one, three, weight=1.0, length=length, tiles=tiles_of(2))
@@ -283,7 +290,7 @@
     flip_field(window, position, count, 1)
     flip_state(one, position, count, 1)
     guards(one, range(3), 2, half)
-    coarse_step((one, two, three), window, lambda n: range(3) if n < 2 else (1,), half, GROUP)
+    coarse_step((one, two, three), window, lambda n: range(3) if n < 2 else (1,), half)
     for k in range(half):
         for comp in range(3):
             value = one[1, comp, :, strip(k)]
@@ -324,7 +331,7 @@
             reach = -(-2 * (18 - 3 * s - n - 1) // ROWS)
             return range(5 - reach, 6 + reach)
 
-        coarse_step((one, two, three), window, tiles_of, half, 8)
+        coarse_step((one, two, three), window, tiles_of, half)
         out = outs[s // 2]
         for k in range(half):
             lanes = pl.ds(k * LANES, LANES)
@@ -459,8 +466,7 @@
     q = swap(message, fifth)
     c = swap(message, far_odd)
     a = swap(message, near_odd)
-    a, b, c, d, q, sib, halfway = lax.optimization_barrier((a, b, c, d, q, sib, halfway))
-    arrived = lax.ppermute(halfway, ("tm", "space"), legs[1])
+    a, b, c, d, q, sib = lax.optimization_barrier((a, b, c, d, q, sib))
     others = swap(jnp.concatenate([a, b, c, d], axis=0), sibling)
     powers = call(
         functools.partial(powers_kernel, count, strips),
@@ -469,8 +475,8 @@
         "powers",
         pos, message, sib, a, b, c, d, q, others,
     )
-    powers, arrived = lax.optimization_barrier((powers, arrived))
     own = sum(later(x, 2 * d + 2) for d, x in enumerate(powers))
+    arrived = lax.ppermute(halfway, ("tm", "space"), legs[1])
     other = later(own[1:], 1)
     (new_start,) = call(
         functools.partial(final_kernel, strips),

time: 141 us -> 145 us (1.028)
  the two profiles are of different devices: /device:TPU:28 before, /device:TPU:10 now
where the time goes in v3:
time: 145 us; the launch traced here: 144 us
  starting transfers between devices  76.5 us (53%)
  waiting for transfers between devices  33.2 us (23%)
  Pallas kernels  32.4 us (22%)
    ppermute x13, starting transfers between devices, swap(): return lax.ppermute(block, 'space', pairs)  53.7 us
    pallas_call x4, Pallas kernels, call(): pl.pallas_call(kernel, out_shape=outs, in_specs=[SMEM] + [VMEM] * (len(ar...  32.4 us
    ppermute x13, waiting for transfers between devices, swap(): return lax.ppermute(block, 'space', pairs)  17 us
    ppermute x1, starting transfers between devices, body(): arrived = lax.ppermute(halfway, ('tm', 'space'), legs[1])  13.6 us
    ppermute x4, waiting for transfers between devices, later(): lax.ppermute(block, 'tm', [(m, m + distance) for m in range(slices - dist...  8.89 us
    ppermute x4, starting transfers between devices, later(): lax.ppermute(block, 'tm', [(m, m + distance) for m in range(slices - dist...  7.37 us
    ppermute x1, waiting for transfers between devices, body(): arrived = lax.ppermute(halfway, ('tm', 'space'), legs[1])  7.34 us
  transfers between devices with their start and end apart: 19, of which 6 were waited for; matrix products, arithmetic and copies ran while one was open for 0% of the time, Pallas kernels for 9%

profile of v3, /device:TPU:10, one launch (start us, length us, event | category | flops | bytes accessed | tf_op | source)
XLA Modules:
  0.0 144.2 jit_solution(10065905864158510864)
XLA Ops:
  1.7 11.2 %collective-permute-start.2 = (f32[4,8,2048]{2,1,0:T(8,128)S(1)}, f32[4,8,2048]{2,1,0:T(8,128)S(1)}, u32[]{:S(2)}, u32[]{:S(2)}) collective-permute-start(f32[4,8,2048]{2,1,0:T(8,128)S(1)} %pad_maximum_fusion), channel_id=1, source_target_pairs={{1,4},{3,6},{4,1},{5,8},{6,3},{7,10},{8,5},{9,12},{10,7},{11,14},{... | collective-permute-start | bytes 786440 | tf_op jit(solution)/shard_map/ppermute | solution.py:377
  12.9 3.8 %collective-permute-start.1 = (f32[4,8,2048]{2,1,0:T(8,128)S(1)}, f32[4,8,2048]{2,1,0:T(8,128)S(1)}, u32[]{:S(2)}, u32[]{:S(2)}) collective-permute-start(f32[4,8,2048]{2,1,0:T(8,128)S(1)} %pad_maximum_fusion), channel_id=1, source_target_pairs={{0,2},{1,3},{2,0},{3,1},{4,6},{5,7},{6,4},{7,5},{8,10},{9,11},{10,... | collective-permute-start | bytes 786440 | tf_op jit(solution)/shard_map/ppermute | solution.py:377
  16.7 2.0 %collective-permute-start = (f32[4,8,2048]{2,1,0:T(8,128)S(1)}, f32[4,8,2048]{2,1,0:T(8,128)S(1)}, u32[]{:S(2)}, u32[]{:S(2)}) collective-permute-start(f32[4,8,2048]{2,1,0:T(8,128)S(1)} %pad_maximum_fusion), channel_id=1, source_target_pairs={{2,4},{3,5},{4,2},{5,3},{6,8},{7,9},{8,6},{9,7},{10,12},{11,13},{1... | collective-permute-start | bytes 786440 | tf_op jit(solution)/shard_map/ppermute | solution.py:377
  18.8 1.9 %collective-permute-start.3 = (f32[4,8,2048]{2,1,0:T(8,128)S(1)}, f32[4,8,2048]{2,1,0:T(8,128)S(1)}, u32[]{:S(2)}, u32[]{:S(2)}) collective-permute-start(f32[4,8,2048]{2,1,0:T(8,128)S(1)} %pad_maximum_fusion), channel_id=1, source_target_pairs={{0,1},{1,0},{2,3},{3,2},{4,5},{5,4},{6,7},{7,6},{8,9},{9,8},{10,11... | collective-permute-start | bytes 786440 | tf_op jit(solution)/shard_map/ppermute | solution.py:377
  20.7 3.9 %collective-permute-done.2.third = f32[4,8,2048]{2,1,0:T(8,128)S(1)} collective-permute-done((f32[4,8,2048]{2,1,0:T(8,128)S(1)}, f32[4,8,2048]{2,1,0:T(8,128)S(1)}, u32[]{:S(2)}, u32[]{:S(2)}) %collective-permute-start.2) | collective-permute-done | bytes 262176 | tf_op jit(solution)/shard_map/ppermute | solution.py:377
  24.6 8.0 %collective-permute-done.near_a = f32[4,8,2048]{2,1,0:T(8,128)S(1)} collective-permute-done((f32[4,8,2048]{2,1,0:T(8,128)S(1)}, f32[4,8,2048]{2,1,0:T(8,128)S(1)}, u32[]{:S(2)}, u32[]{:S(2)}) %collective-permute-start) | collective-permute-done | bytes 262176 | tf_op jit(solution)/shard_map/ppermute | solution.py:377
  34.6 2.4 %collective-permute-start.5 = (f32[4,8,2048]{2,1,0:T(8,128)S(1)}, f32[4,8,2048]{2,1,0:T(8,128)S(1)}, u32[]{:S(2)}, u32[]{:S(2)}) collective-permute-start(f32[4,8,2048]{2,1,0:T(8,128)S(1)} %collective-permute-done.1.near_b), channel_id=1, source_target_pairs={{0,1},{1,0},{2,3},{3,2},{4,5},{5,4},{6,7},{7,6},{8,9},{9,8},{10,11... | collective-permute-start | bytes 786440 | tf_op jit(solution)/shard_map/ppermute | solution.py:377
  38.1 2.4 %coarse.1 = (f32[3,8,2048]{2,1,0:T(8,128)}, f32[3,8,1024]{2,1,0:T(8,128)S(1)}) custom-call(s32[2]{0:T(128)S(1)} %pad_add_fusion.pos, f32[3,8,2048]{2,1,0:T(8,128)S(1)} %bitcast.8, f32[8,2048]{1,0:T(8,128)S(1)} %copy-done.1, f32[4,8,2048]{2,1,0:T(8,128)S(1)} %collective-permute-done.3.sib, f32[4,8,2048]{2,1,0:T(8,128)S(1)} %collective-permute-done.4.sib_a, ...), custom_call_target="tpu_custom_call" | custom-call | tf_op jit(solution)/shard_map/coarse/pallas_call | solution.py:362
  40.6 15.5 %fine.1 = (f32[3,8,2048]{2,1,0:T(8,128)}, f32[3,8,2048]{2,1,0:T(8,128)S(1)}, f32[2,8,1024]{2,1,0:T(8,128)S(1)}) custom-call(s32[2]{0:T(128)S(1)} %pad_add_fusion.pos, f32[3,8,2048]{2,1,0:T(8,128)S(1)} %bitcast.9, f32[8,2048]{1,0:T(8,128)S(1)} %copy-done.1, f32[4,8,2048]{2,1,0:T(8,128)S(1)} %collective-permute-done.near_a, ...), custom_call_target="tpu_custom_call" | custom-call | tf_op jit(solution)/shard_map/fine/pallas_call | solution.py:362
  56.1 2.3 %collective-permute-start.11 = (f32[2,8,1024]{2,1,0:T(8,128)S(1)}, f32[2,8,1024]{2,1,0:T(8,128)S(1)}, u32[]{:S(2)}, u32[]{:S(2)}) collective-permute-start(f32[2,8,1024]{2,1,0:T(8,128)S(1)} %get-tuple-element.24.own), channel_id=1, source_target_pairs={{0,1},{1,0},{2,3},{3,2},{4,5},{5,4},{6,7},{7,6},{8,9},{9,8},{10,11... | collective-permute-start | bytes 196616 | tf_op jit(solution)/shard_map/ppermute | solution.py:377
  58.4 6.2 %collective-permute-start.10 = (f32[2,8,1024]{2,1,0:T(8,128)S(1)}, f32[2,8,1024]{2,1,0:T(8,128)S(1)}, u32[]{:S(2)}, u32[]{:S(2)}) collective-permute-start(f32[2,8,1024]{2,1,0:T(8,128)S(1)} %get-tuple-element.24.own), channel_id=1, source_target_pairs={{1,6},{3,8},{5,10},{6,1},{7,12},{8,3},{9,14},{10,5},{11,16},{12,7}... | collective-permute-start | bytes 196616 | tf_op jit(solution)/shard_map/ppermute | solution.py:377
  64.6 2.9 %collective-permute-start.9 = (f32[2,8,1024]{2,1,0:T(8,128)S(1)}, f32[2,8,1024]{2,1,0:T(8,128)S(1)}, u32[]{:S(2)}, u32[]{:S(2)}) collective-permute-start(f32[2,8,1024]{2,1,0:T(8,128)S(1)} %get-tuple-element.24.own), channel_id=1, source_target_pairs={{0,4},{1,5},{2,6},{3,7},{4,0},{5,1},{6,2},{7,3},{8,12},{9,13},{10,... | collective-permute-start | bytes 196616 | tf_op jit(solution)/shard_map/ppermute | solution.py:377
  67.5 3.5 %collective-permute-start.8 = (f32[2,8,1024]{2,1,0:T(8,128)S(1)}, f32[2,8,1024]{2,1,0:T(8,128)S(1)}, u32[]{:S(2)}, u32[]{:S(2)}) collective-permute-start(f32[2,8,1024]{2,1,0:T(8,128)S(1)} %get-tuple-element.24.own), channel_id=1, source_target_pairs={{4,8},{5,9},{6,10},{7,11},{8,4},{9,5},{10,6},{11,7},{12,16},{13,17... | collective-permute-start | bytes 196616 | tf_op jit(solution)/shard_map/ppermute | solution.py:377
  71.0 2.7 %collective-permute-start.7 = (f32[2,8,1024]{2,1,0:T(8,128)S(1)}, f32[2,8,1024]{2,1,0:T(8,128)S(1)}, u32[]{:S(2)}, u32[]{:S(2)}) collective-permute-start(f32[2,8,1024]{2,1,0:T(8,128)S(1)} %get-tuple-element.24.own), channel_id=1, source_target_pairs={{0,2},{1,3},{2,0},{3,1},{4,6},{5,7},{6,4},{7,5},{8,10},{9,11},{10,... | collective-permute-start | bytes 196616 | tf_op jit(solution)/shard_map/ppermute | solution.py:377
  73.7 9.6 %collective-permute-start.6 = (f32[2,8,1024]{2,1,0:T(8,128)S(1)}, f32[2,8,1024]{2,1,0:T(8,128)S(1)}, u32[]{:S(2)}, u32[]{:S(2)}) collective-permute-start(f32[2,8,1024]{2,1,0:T(8,128)S(1)} %get-tuple-element.24.own), channel_id=1, source_target_pairs={{2,4},{3,5},{4,2},{5,3},{6,8},{7,9},{8,6},{9,7},{10,12},{11,13},{1... | collective-permute-start | bytes 196616 | tf_op jit(solution)/shard_map/ppermute | solution.py:377
  83.4 4.0 %collective-permute-done.6.near_a = f32[2,8,1024]{2,1,0:T(8,128)S(1)} collective-permute-done((f32[2,8,1024]{2,1,0:T(8,128)S(1)}, f32[2,8,1024]{2,1,0:T(8,128)S(1)}, u32[]{:S(2)}, u32[]{:S(2)}) %collective-permute-start.6) | collective-permute-done | bytes 65568 | tf_op jit(solution)/shard_map/ppermute | solution.py:377
  87.4 3.2 %collective-permute-start.12 = (f32[8,8,1024]{2,1,0:T(8,128)S(1)}, f32[8,8,1024]{2,1,0:T(8,128)S(1)}, u32[]{:S(2)}, u32[]{:S(2)}) collective-permute-start(f32[8,8,1024]{2,1,0:T(8,128)S(1)} %pad_maximum_fusion.1), channel_id=1, source_target_pairs={{0,1},{1,0},{2,3},{3,2},{4,5},{5,4},{6,7},{7,6},{8,9},{9,8},{10,11... | collective-permute-start | bytes 786440 | tf_op jit(solution)/shard_map/ppermute | solution.py:377
  90.6 1.9 %collective-permute-start.17 = (f32[3,8,2048]{2,1,0:T(8,128)S(1)}, f32[3,8,2048]{2,1,0:T(8,128)S(1)}, u32[]{:S(2)}, u32[]{:S(2)}) collective-permute-start(f32[3,8,2048]{2,1,0:T(8,128)S(1)} %get-tuple-element.34), channel_id=1, source_target_pairs={{0,8},{1,73},{2,10},{3,75},{4,12},{5,77},{6,14},{7,79},{8,64},{9,1... | collective-permute-start | bytes 589832 | tf_op jit(solution)/shard_map/ppermute | solution.py:462
  92.5 13.1 %powers.1 = (f32[3,8,1024]{2,1,0:T(8,128)S(1)}, f32[3,8,1024]{2,1,0:T(8,128)S(1)}, f32[3,8,1024]{2,1,0:T(8,128)S(1)}) custom-call(s32[2]{0:T(128)S(1)} %pad_add_fusion.pos, f32[2,8,1024]{2,1,0:T(8,128)S(1)} %get-tuple-element.24.own, f32[2,8,1024]{2,1,0:T(8,128)S(1)} %collective-permute-done.11.sib, f32[2,8,1024]{2,1,0:T(8,128)S(1)} %collective-permute-done.6.near_a, ...), custom_call_target="tpu_custom_call" | custom-call | tf_op jit(solution)/shard_map/powers/pallas_call | solution.py:362
  105.6 3.5 %collective-permute-start.13 = (f32[3,8,1024]{2,1,0:T(8,128)S(1)}, f32[3,8,1024]{2,1,0:T(8,128)S(1)}, u32[]{:S(2)}, u32[]{:S(2)}) collective-permute-start(f32[3,8,1024]{2,1,0:T(8,128)S(1)} %get-tuple-element.31), channel_id=1, source_target_pairs={{0,128},{64,192},{128,256},{192,320},{256,384},{320,448},{1,129},{... | collective-permute-start | bytes 294920 | tf_op jit(solution)/shard_map/ppermute | solution.py:382
  111.1 13.6 %collective-permute-start.18 = (f32[3,8,2048]{2,1,0:T(8,128)S(1)}, f32[3,8,2048]{2,1,0:T(8,128)S(1)}, u32[]{:S(2)}, u32[]{:S(2)}) collective-permute-start(f32[3,8,2048]{2,1,0:T(8,128)S(1)} %collective-permute-done.17), channel_id=1, source_target_pairs={{8,64},{73,65},{10,66},{75,67},{12,68},{77,69},{14,70},{79,71},{64... | collective-permute-start | bytes 589832 | tf_op jit(solution)/shard_map/ppermute | solution.py:479
  124.8 1.9 %collective-permute-start.16 = (f32[2,8,1024]{2,1,0:T(8,128)S(1)}, f32[2,8,1024]{2,1,0:T(8,128)S(1)}, u32[]{:S(2)}, u32[]{:S(2)}) collective-permute-start(f32[2,8,1024]{2,1,0:T(8,128)S(1)} %slice.4), channel_id=1, source_target_pairs={{0,64},{64,128},{128,192},{192,256},{256,320},{320,384},{384,448},... | collective-permute-start | bytes 196616 | tf_op jit(solution)/shard_map/ppermute | solution.py:382
  126.7 7.3 %collective-permute-done.18.detail = f32[3,8,2048]{2,1,0:T(8,128)S(1)} collective-permute-done((f32[3,8,2048]{2,1,0:T(8,128)S(1)}, f32[3,8,2048]{2,1,0:T(8,128)S(1)}, u32[]{:S(2)}, u32[]{:S(2)}) %collective-permute-start.18) | collective-permute-done | bytes 196640 | tf_op jit(solution)/shard_map/ppermute | solution.py:479
  134.0 8.9 %collective-permute-done.16.other = f32[2,8,1024]{2,1,0:T(8,128)S(1)} collective-permute-done((f32[2,8,1024]{2,1,0:T(8,128)S(1)}, f32[2,8,1024]{2,1,0:T(8,128)S(1)}, u32[]{:S(2)}, u32[]{:S(2)}) %collective-permute-start.16) | collective-permute-done | bytes 65568 | tf_op jit(solution)/shard_map/ppermute | solution.py:382
  (27 shorter events, 7.4 us)
Async XLA Ops:
  0.6 37.5 %copy-start = (f32[1,3,8,2048]{3,2,1,0:T(8,128)S(1)}, f32[1,3,8,2048]{3,2,1,0:T(8,128)}, u32[]{:S(2)}) copy-start(f32[1,3,8,2048]{3,2,1,0:T(8,128)} %param.2) | copy-start | bytes 589828
  0.6 37.5 %copy-start.1 = (f32[8,2048]{1,0:T(8,128)S(1)}, f32[8,2048]{1,0:T(8,128)}, u32[]{:S(2)}) copy-start(f32[8,2048]{1,0:T(8,128)} %field.3) | copy-start | bytes 196612
  1.7 23.0 %collective-permute-start.2 = (f32[4,8,2048]{2,1,0:T(8,128)S(1)}, f32[4,8,2048]{2,1,0:T(8,128)S(1)}, u32[]{:S(2)}, u32[]{:S(2)}) collective-permute-start(f32[4,8,2048]{2,1,0:T(8,128)S(1)} %pad_maximum_fusion), channel_id=1, source_target_pairs={{1,4},{3,6},{4,1},{5,8},{6,3},{7,10},{8,5},{9,12},{10,7},{11,14},{... | collective-permute-start | bytes 786440 | tf_op jit(solution)/shard_map/ppermute | solution.py:377
  12.9 11.7 %collective-permute-start.1 = (f32[4,8,2048]{2,1,0:T(8,128)S(1)}, f32[4,8,2048]{2,1,0:T(8,128)S(1)}, u32[]{:S(2)}, u32[]{:S(2)}) collective-permute-start(f32[4,8,2048]{2,1,0:T(8,128)S(1)} %pad_maximum_fusion), channel_id=1, source_target_pairs={{0,2},{1,3},{2,0},{3,1},{4,6},{5,7},{6,4},{7,5},{8,10},{9,11},{10,... | collective-permute-start | bytes 786440 | tf_op jit(solution)/shard_map/ppermute | solution.py:377
  16.7 15.9 %collective-permute-start = (f32[4,8,2048]{2,1,0:T(8,128)S(1)}, f32[4,8,2048]{2,1,0:T(8,128)S(1)}, u32[]{:S(2)}, u32[]{:S(2)}) collective-permute-start(f32[4,8,2048]{2,1,0:T(8,128)S(1)} %pad_maximum_fusion), channel_id=1, source_target_pairs={{2,4},{3,5},{4,2},{5,3},{6,8},{7,9},{8,6},{9,7},{10,12},{11,13},{1... | collective-permute-start | bytes 786440 | tf_op jit(solution)/shard_map/ppermute | solution.py:377
  18.8 18.3 %collective-permute-start.3 = (f32[4,8,2048]{2,1,0:T(8,128)S(1)}, f32[4,8,2048]{2,1,0:T(8,128)S(1)}, u32[]{:S(2)}, u32[]{:S(2)}) collective-permute-start(f32[4,8,2048]{2,1,0:T(8,128)S(1)} %pad_maximum_fusion), channel_id=1, source_target_pairs={{0,1},{1,0},{2,3},{3,2},{4,5},{5,4},{6,7},{7,6},{8,9},{9,8},{10,11... | collective-permute-start | bytes 786440 | tf_op jit(solution)/shard_map/ppermute | solution.py:377
  32.7 4.4 %collective-permute-start.4 = (f32[4,8,2048]{2,1,0:T(8,128)S(1)}, f32[4,8,2048]{2,1,0:T(8,128)S(1)}, u32[]{:S(2)}, u32[]{:S(2)}) collective-permute-start(f32[4,8,2048]{2,1,0:T(8,128)S(1)} %collective-permute-done.near_a), channel_id=1, source_target_pairs={{0,1},{1,0},{2,3},{3,2},{4,5},{5,4},{6,7},{7,6},{8,9},{9,8},{10,11... | collective-permute-start | bytes 786440 | tf_op jit(solution)/shard_map/ppermute | solution.py:377
  34.6 3.6 %collective-permute-start.5 = (f32[4,8,2048]{2,1,0:T(8,128)S(1)}, f32[4,8,2048]{2,1,0:T(8,128)S(1)}, u32[]{:S(2)}, u32[]{:S(2)}) collective-permute-start(f32[4,8,2048]{2,1,0:T(8,128)S(1)} %collective-permute-done.1.near_b), channel_id=1, source_target_pairs={{0,1},{1,0},{2,3},{3,2},{4,5},{5,4},{6,7},{7,6},{8,9},{9,8},{10,11... | collective-permute-start | bytes 786440 | tf_op jit(solution)/shard_map/ppermute | solution.py:377
  56.1 17.6 %collective-permute-start.11 = (f32[2,8,1024]{2,1,0:T(8,128)S(1)}, f32[2,8,1024]{2,1,0:T(8,128)S(1)}, u32[]{:S(2)}, u32[]{:S(2)}) collective-permute-start(f32[2,8,1024]{2,1,0:T(8,128)S(1)} %get-tuple-element.24.own), channel_id=1, source_target_pairs={{0,1},{1,0},{2,3},{3,2},{4,5},{5,4},{6,7},{7,6},{8,9},{9,8},{10,11... | collective-permute-start | bytes 196616 | tf_op jit(solution)/shard_map/ppermute | solution.py:377
  58.4 25.0 %collective-permute-start.10 = (f32[2,8,1024]{2,1,0:T(8,128)S(1)}, f32[2,8,1024]{2,1,0:T(8,128)S(1)}, u32[]{:S(2)}, u32[]{:S(2)}) collective-permute-start(f32[2,8,1024]{2,1,0:T(8,128)S(1)} %get-tuple-element.24.own), channel_id=1, source_target_pairs={{1,6},{3,8},{5,10},{6,1},{7,12},{8,3},{9,14},{10,5},{11,16},{12,7}... | collective-permute-start | bytes 196616 | tf_op jit(solution)/shard_map/ppermute | solution.py:377
  64.6 18.7 %collective-permute-start.9 = (f32[2,8,1024]{2,1,0:T(8,128)S(1)}, f32[2,8,1024]{2,1,0:T(8,128)S(1)}, u32[]{:S(2)}, u32[]{:S(2)}) collective-permute-start(f32[2,8,1024]{2,1,0:T(8,128)S(1)} %get-tuple-element.24.own), channel_id=1, source_target_pairs={{0,4},{1,5},{2,6},{3,7},{4,0},{5,1},{6,2},{7,3},{8,12},{9,13},{10,... | collective-permute-start | bytes 196616 | tf_op jit(solution)/shard_map/ppermute | solution.py:377
  67.5 15.9 %collective-permute-start.8 = (f32[2,8,1024]{2,1,0:T(8,128)S(1)}, f32[2,8,1024]{2,1,0:T(8,128)S(1)}, u32[]{:S(2)}, u32[]{:S(2)}) collective-permute-start(f32[2,8,1024]{2,1,0:T(8,128)S(1)} %get-tuple-element.24.own), channel_id=1, source_target_pairs={{4,8},{5,9},{6,10},{7,11},{8,4},{9,5},{10,6},{11,7},{12,16},{13,17... | collective-permute-start | bytes 196616 | tf_op jit(solution)/shard_map/ppermute | solution.py:377
  71.0 12.4 %collective-permute-start.7 = (f32[2,8,1024]{2,1,0:T(8,128)S(1)}, f32[2,8,1024]{2,1,0:T(8,128)S(1)}, u32[]{:S(2)}, u32[]{:S(2)}) collective-permute-start(f32[2,8,1024]{2,1,0:T(8,128)S(1)} %get-tuple-element.24.own), channel_id=1, source_target_pairs={{0,2},{1,3},{2,0},{3,1},{4,6},{5,7},{6,4},{7,5},{8,10},{9,11},{10,... | collective-permute-start | bytes 196616 | tf_op jit(solution)/shard_map/ppermute | solution.py:377
  73.7 13.7 %collective-permute-start.6 = (f32[2,8,1024]{2,1,0:T(8,128)S(1)}, f32[2,8,1024]{2,1,0:T(8,128)S(1)}, u32[]{:S(2)}, u32[]{:S(2)}) collective-permute-start(f32[2,8,1024]{2,1,0:T(8,128)S(1)} %get-tuple-element.24.own), channel_id=1, source_target_pairs={{2,4},{3,5},{4,2},{5,3},{6,8},{7,9},{8,6},{9,7},{10,12},{11,13},{1... | collective-permute-start | bytes 196616 | tf_op jit(solution)/shard_map/ppermute | solution.py:377
  87.4 5.1 %collective-permute-start.12 = (f32[8,8,1024]{2,1,0:T(8,128)S(1)}, f32[8,8,1024]{2,1,0:T(8,128)S(1)}, u32[]{:S(2)}, u32[]{:S(2)}) collective-permute-start(f32[8,8,1024]{2,1,0:T(8,128)S(1)} %pad_maximum_fusion.1), channel_id=1, source_target_pairs={{0,1},{1,0},{2,3},{3,2},{4,5},{5,4},{6,7},{7,6},{8,9},{9,8},{10,11... | collective-permute-start | bytes 786440 | tf_op jit(solution)/shard_map/ppermute | solution.py:377
  90.6 20.5 %collective-permute-start.17 = (f32[3,8,2048]{2,1,0:T(8,128)S(1)}, f32[3,8,2048]{2,1,0:T(8,128)S(1)}, u32[]{:S(2)}, u32[]{:S(2)}) collective-permute-start(f32[3,8,2048]{2,1,0:T(8,128)S(1)} %get-tuple-element.34), channel_id=1, source_target_pairs={{0,8},{1,73},{2,10},{3,75},{4,12},{5,77},{6,14},{7,79},{8,64},{9,1... | collective-permute-start | bytes 589832 | tf_op jit(solution)/shard_map/ppermute | solution.py:462
  105.6 19.1 %collective-permute-start.13 = (f32[3,8,1024]{2,1,0:T(8,128)S(1)}, f32[3,8,1024]{2,1,0:T(8,128)S(1)}, u32[]{:S(2)}, u32[]{:S(2)}) collective-permute-start(f32[3,8,1024]{2,1,0:T(8,128)S(1)} %get-tuple-element.31), channel_id=1, source_target_pairs={{0,128},{64,192},{128,256},{192,320},{256,384},{320,448},{1,129},{... | collective-permute-start | bytes 294920 | tf_op jit(solution)/shard_map/ppermute | solution.py:382
  109.1 15.6 %collective-permute-start.14 = (f32[3,8,1024]{2,1,0:T(8,128)S(1)}, f32[3,8,1024]{2,1,0:T(8,128)S(1)}, u32[]{:S(2)}, u32[]{:S(2)}) collective-permute-start(f32[3,8,1024]{2,1,0:T(8,128)S(1)} %get-tuple-element.32), channel_id=1, source_target_pairs={{0,256},{64,320},{128,384},{192,448},{1,257},{65,321},{129,385},{1... | collective-permute-start | bytes 294920 | tf_op jit(solution)/shard_map/ppermute | solution.py:382
  110.4 14.3 %collective-permute-start.15 = (f32[3,8,1024]{2,1,0:T(8,128)S(1)}, f32[3,8,1024]{2,1,0:T(8,128)S(1)}, u32[]{:S(2)}, u32[]{:S(2)}) collective-permute-start(f32[3,8,1024]{2,1,0:T(8,128)S(1)} %get-tuple-element.33), channel_id=1, source_target_pairs={{0,384},{64,448},{1,385},{65,449},{2,386},{66,450},{3,387},{67,451... | collective-permute-start | bytes 294920 | tf_op jit(solution)/shard_map/ppermute | solution.py:382
  111.1 22.9 %collective-permute-start.18 = (f32[3,8,2048]{2,1,0:T(8,128)S(1)}, f32[3,8,2048]{2,1,0:T(8,128)S(1)}, u32[]{:S(2)}, u32[]{:S(2)}) collective-permute-start(f32[3,8,2048]{2,1,0:T(8,128)S(1)} %collective-permute-done.17), channel_id=1, source_target_pairs={{8,64},{73,65},{10,66},{75,67},{12,68},{77,69},{14,70},{79,71},{64... | collective-permute-start | bytes 589832 | tf_op jit(solution)/shard_map/ppermute | solution.py:479
  124.8 18.1 %collective-permute-start.16 = (f32[2,8,1024]{2,1,0:T(8,128)S(1)}, f32[2,8,1024]{2,1,0:T(8,128)S(1)}, u32[]{:S(2)}, u32[]{:S(2)}) collective-permute-start(f32[2,8,1024]{2,1,0:T(8,128)S(1)} %slice.4), channel_id=1, source_target_pairs={{0,64},{64,128},{128,192},{192,256},{256,320},{320,384},{384,448},... | collective-permute-start | bytes 196616 | tf_op jit(solution)/shard_map/ppermute | solution.py:382

commit v4 on v2

--- a/solution.py
+++ b/solution.py
@@ -459,8 +459,7 @@
     q = swap(message, fifth)
     c = swap(message, far_odd)
     a = swap(message, near_odd)
-    a, b, c, d, q, sib, halfway = lax.optimization_barrier((a, b, c, d, q, sib, halfway))
-    arrived = lax.ppermute(halfway, ("tm", "space"), legs[1])
+    a, b, c, d, q, sib = lax.optimization_barrier((a, b, c, d, q, sib))
     others = swap(jnp.concatenate([a, b, c, d], axis=0), sibling)
     powers = call(
         functools.partial(powers_kernel, count, strips),
@@ -469,8 +468,8 @@
         "powers",
         pos, message, sib, a, b, c, d, q, others,
     )
-    powers, arrived = lax.optimization_barrier((powers, arrived))
     own = sum(later(x, 2 * d + 2) for d, x in enumerate(powers))
+    arrived = lax.ppermute(halfway, ("tm", "space"), legs[1])
     other = later(own[1:], 1)
     (new_start,) = call(
         functools.partial(final_kernel, strips),

time: 141 us -> 135 us (0.957)
  the two profiles are of different devices: /device:TPU:28 before, /device:TPU:10 now
where the time goes in v4:
time: 135 us
  starting transfers between devices  76.5 us (57%)
  waiting for transfers between devices  33.2 us (25%)
  Pallas kernels  22.8 us (17%)
    ppermute x13, starting transfers between devices, swap(): return lax.ppermute(block, 'space', pairs)  53.7 us
    pallas_call x4, Pallas kernels, call(): pl.pallas_call(kernel, out_shape=outs, in_specs=[SMEM] + [VMEM] * (len(ar...  22.8 us
    ppermute x13, waiting for transfers between devices, swap(): return lax.ppermute(block, 'space', pairs)  17 us
    ppermute x1, starting transfers between devices, body(): arrived = lax.ppermute(halfway, ('tm', 'space'), legs[1])  13.6 us
    ppermute x4, waiting for transfers between devices, later(): lax.ppermute(block, 'tm', [(m, m + distance) for m in range(slices - dist...  8.89 us
    ppermute x4, starting transfers between devices, later(): lax.ppermute(block, 'tm', [(m, m + distance) for m in range(slices - dist...  7.37 us
    ppermute x1, waiting for transfers between devices, body(): arrived = lax.ppermute(halfway, ('tm', 'space'), legs[1])  7.34 us
  transfers between devices with their start and end apart: 19, of which 6 were waited for; matrix products, arithmetic and copies ran while one was open for 0% of the time, Pallas kernels for 5%

profile of v4, /device:TPU:10, one launch (start us, length us, event | category | flops | bytes accessed | tf_op | source)
XLA Modules:
  0.0 134.6 jit_solution(11327819978916915142)
XLA Ops:
  1.7 11.2 %collective-permute-start.2 = (f32[4,8,2048]{2,1,0:T(8,128)S(1)}, f32[4,8,2048]{2,1,0:T(8,128)S(1)}, u32[]{:S(2)}, u32[]{:S(2)}) collective-permute-start(f32[4,8,2048]{2,1,0:T(8,128)S(1)} %pad_maximum_fusion), channel_id=1, source_target_pairs={{1,4},{3,6},{4,1},{5,8},{6,3},{7,10},{8,5},{9,12},{10,7},{11,14},{... | collective-permute-start | bytes 786440 | tf_op jit(solution)/shard_map/ppermute | solution.py:370
  12.9 3.8 %collective-permute-start.1 = (f32[4,8,2048]{2,1,0:T(8,128)S(1)}, f32[4,8,2048]{2,1,0:T(8,128)S(1)}, u32[]{:S(2)}, u32[]{:S(2)}) collective-permute-start(f32[4,8,2048]{2,1,0:T(8,128)S(1)} %pad_maximum_fusion), channel_id=1, source_target_pairs={{0,2},{1,3},{2,0},{3,1},{4,6},{5,7},{6,4},{7,5},{8,10},{9,11},{10,... | collective-permute-start | bytes 786440 | tf_op jit(solution)/shard_map/ppermute | solution.py:370
  16.7 2.0 %collective-permute-start = (f32[4,8,2048]{2,1,0:T(8,128)S(1)}, f32[4,8,2048]{2,1,0:T(8,128)S(1)}, u32[]{:S(2)}, u32[]{:S(2)}) collective-permute-start(f32[4,8,2048]{2,1,0:T(8,128)S(1)} %pad_maximum_fusion), channel_id=1, source_target_pairs={{2,4},{3,5},{4,2},{5,3},{6,8},{7,9},{8,6},{9,7},{10,12},{11,13},{1... | collective-permute-start | bytes 786440 | tf_op jit(solution)/shard_map/ppermute | solution.py:370
  18.8 1.9 %collective-permute-start.3 = (f32[4,8,2048]{2,1,0:T(8,128)S(1)}, f32[4,8,2048]{2,1,0:T(8,128)S(1)}, u32[]{:S(2)}, u32[]{:S(2)}) collective-permute-start(f32[4,8,2048]{2,1,0:T(8,128)S(1)} %pad_maximum_fusion), channel_id=1, source_target_pairs={{0,1},{1,0},{2,3},{3,2},{4,5},{5,4},{6,7},{7,6},{8,9},{9,8},{10,11... | collective-permute-start | bytes 786440 | tf_op jit(solution)/shard_map/ppermute | solution.py:370
  20.7 3.9 %collective-permute-done.2.third = f32[4,8,2048]{2,1,0:T(8,128)S(1)} collective-permute-done((f32[4,8,2048]{2,1,0:T(8,128)S(1)}, f32[4,8,2048]{2,1,0:T(8,128)S(1)}, u32[]{:S(2)}, u32[]{:S(2)}) %collective-permute-start.2) | collective-permute-done | bytes 262176 | tf_op jit(solution)/shard_map/ppermute | solution.py:370
  24.6 8.0 %collective-permute-done.near_a = f32[4,8,2048]{2,1,0:T(8,128)S(1)} collective-permute-done((f32[4,8,2048]{2,1,0:T(8,128)S(1)}, f32[4,8,2048]{2,1,0:T(8,128)S(1)}, u32[]{:S(2)}, u32[]{:S(2)}) %collective-permute-start) | collective-permute-done | bytes 262176 | tf_op jit(solution)/shard_map/ppermute | solution.py:370
  34.6 2.4 %collective-permute-start.5 = (f32[4,8,2048]{2,1,0:T(8,128)S(1)}, f32[4,8,2048]{2,1,0:T(8,128)S(1)}, u32[]{:S(2)}, u32[]{:S(2)}) collective-permute-start(f32[4,8,2048]{2,1,0:T(8,128)S(1)} %collective-permute-done.1.near_b), channel_id=1, source_target_pairs={{0,1},{1,0},{2,3},{3,2},{4,5},{5,4},{6,7},{7,6},{8,9},{9,8},{10,11... | collective-permute-start | bytes 786440 | tf_op jit(solution)/shard_map/ppermute | solution.py:370
  38.1 2.4 %coarse.1 = (f32[3,8,2048]{2,1,0:T(8,128)}, f32[3,8,1024]{2,1,0:T(8,128)S(1)}) custom-call(s32[2]{0:T(128)S(1)} %pad_add_fusion.pos, f32[3,8,2048]{2,1,0:T(8,128)S(1)} %bitcast.8, f32[8,2048]{1,0:T(8,128)S(1)} %copy-done.1, f32[4,8,2048]{2,1,0:T(8,128)S(1)} %collective-permute-done.3.sib, f32[4,8,2048]{2,1,0:T(8,128)S(1)} %collective-permute-done.4.sib_a, ...), custom_call_target="tpu_custom_call" | custom-call | tf_op jit(solution)/shard_map/coarse/pallas_call | solution.py:355
  40.6 12.0 %fine.1 = (f32[3,8,2048]{2,1,0:T(8,128)}, f32[3,8,2048]{2,1,0:T(8,128)S(1)}, f32[2,8,1024]{2,1,0:T(8,128)S(1)}) custom-call(s32[2]{0:T(128)S(1)} %pad_add_fusion.pos, f32[3,8,2048]{2,1,0:T(8,128)S(1)} %bitcast.9, f32[8,2048]{1,0:T(8,128)S(1)} %copy-done.1, f32[4,8,2048]{2,1,0:T(8,128)S(1)} %collective-permute-done.near_a, ...), custom_call_target="tpu_custom_call" | custom-call | tf_op jit(solution)/shard_map/fine/pallas_call | solution.py:355
  52.5 2.3 %collective-permute-start.11 = (f32[2,8,1024]{2,1,0:T(8,128)S(1)}, f32[2,8,1024]{2,1,0:T(8,128)S(1)}, u32[]{:S(2)}, u32[]{:S(2)}) collective-permute-start(f32[2,8,1024]{2,1,0:T(8,128)S(1)} %get-tuple-element.24.own), channel_id=1, source_target_pairs={{0,1},{1,0},{2,3},{3,2},{4,5},{5,4},{6,7},{7,6},{8,9},{9,8},{10,11... | collective-permute-start | bytes 196616 | tf_op jit(solution)/shard_map/ppermute | solution.py:370
  54.8 6.2 %collective-permute-start.10 = (f32[2,8,1024]{2,1,0:T(8,128)S(1)}, f32[2,8,1024]{2,1,0:T(8,128)S(1)}, u32[]{:S(2)}, u32[]{:S(2)}) collective-permute-start(f32[2,8,1024]{2,1,0:T(8,128)S(1)} %get-tuple-element.24.own), channel_id=1, source_target_pairs={{1,6},{3,8},{5,10},{6,1},{7,12},{8,3},{9,14},{10,5},{11,16},{12,7}... | collective-permute-start | bytes 196616 | tf_op jit(solution)/shard_map/ppermute | solution.py:370
  61.1 2.9 %collective-permute-start.9 = (f32[2,8,1024]{2,1,0:T(8,128)S(1)}, f32[2,8,1024]{2,1,0:T(8,128)S(1)}, u32[]{:S(2)}, u32[]{:S(2)}) collective-permute-start(f32[2,8,1024]{2,1,0:T(8,128)S(1)} %get-tuple-element.24.own), channel_id=1, source_target_pairs={{0,4},{1,5},{2,6},{3,7},{4,0},{5,1},{6,2},{7,3},{8,12},{9,13},{10,... | collective-permute-start | bytes 196616 | tf_op jit(solution)/shard_map/ppermute | solution.py:370
  63.9 3.5 %collective-permute-start.8 = (f32[2,8,1024]{2,1,0:T(8,128)S(1)}, f32[2,8,1024]{2,1,0:T(8,128)S(1)}, u32[]{:S(2)}, u32[]{:S(2)}) collective-permute-start(f32[2,8,1024]{2,1,0:T(8,128)S(1)} %get-tuple-element.24.own), channel_id=1, source_target_pairs={{4,8},{5,9},{6,10},{7,11},{8,4},{9,5},{10,6},{11,7},{12,16},{13,17... | collective-permute-start | bytes 196616 | tf_op jit(solution)/shard_map/ppermute | solution.py:370
  67.4 2.7 %collective-permute-start.7 = (f32[2,8,1024]{2,1,0:T(8,128)S(1)}, f32[2,8,1024]{2,1,0:T(8,128)S(1)}, u32[]{:S(2)}, u32[]{:S(2)}) collective-permute-start(f32[2,8,1024]{2,1,0:T(8,128)S(1)} %get-tuple-element.24.own), channel_id=1, source_target_pairs={{0,2},{1,3},{2,0},{3,1},{4,6},{5,7},{6,4},{7,5},{8,10},{9,11},{10,... | collective-permute-start | bytes 196616 | tf_op jit(solution)/shard_map/ppermute | solution.py:370
  70.1 9.6 %collective-permute-start.6 = (f32[2,8,1024]{2,1,0:T(8,128)S(1)}, f32[2,8,1024]{2,1,0:T(8,128)S(1)}, u32[]{:S(2)}, u32[]{:S(2)}) collective-permute-start(f32[2,8,1024]{2,1,0:T(8,128)S(1)} %get-tuple-element.24.own), channel_id=1, source_target_pairs={{2,4},{3,5},{4,2},{5,3},{6,8},{7,9},{8,6},{9,7},{10,12},{11,13},{1... | collective-permute-start | bytes 196616 | tf_op jit(solution)/shard_map/ppermute | solution.py:370
  79.8 4.0 %collective-permute-done.6.near_a = f32[2,8,1024]{2,1,0:T(8,128)S(1)} collective-permute-done((f32[2,8,1024]{2,1,0:T(8,128)S(1)}, f32[2,8,1024]{2,1,0:T(8,128)S(1)}, u32[]{:S(2)}, u32[]{:S(2)}) %collective-permute-start.6) | collective-permute-done | bytes 65568 | tf_op jit(solution)/shard_map/ppermute | solution.py:370
  83.8 3.2 %collective-permute-start.12 = (f32[8,8,1024]{2,1,0:T(8,128)S(1)}, f32[8,8,1024]{2,1,0:T(8,128)S(1)}, u32[]{:S(2)}, u32[]{:S(2)}) collective-permute-start(f32[8,8,1024]{2,1,0:T(8,128)S(1)} %pad_maximum_fusion.1), channel_id=1, source_target_pairs={{0,1},{1,0},{2,3},{3,2},{4,5},{5,4},{6,7},{7,6},{8,9},{9,8},{10,11... | collective-permute-start | bytes 786440 | tf_op jit(solution)/shard_map/ppermute | solution.py:370
  87.0 1.9 %collective-permute-start.17 = (f32[3,8,2048]{2,1,0:T(8,128)S(1)}, f32[3,8,2048]{2,1,0:T(8,128)S(1)}, u32[]{:S(2)}, u32[]{:S(2)}) collective-permute-start(f32[3,8,2048]{2,1,0:T(8,128)S(1)} %get-tuple-element.34), channel_id=1, source_target_pairs={{0,8},{1,73},{2,10},{3,75},{4,12},{5,77},{6,14},{7,79},{8,64},{9,1... | collective-permute-start | bytes 589832 | tf_op jit(solution)/shard_map/ppermute | solution.py:455
  88.9 7.1 %powers.1 = (f32[3,8,1024]{2,1,0:T(8,128)S(1)}, f32[3,8,1024]{2,1,0:T(8,128)S(1)}, f32[3,8,1024]{2,1,0:T(8,128)S(1)}) custom-call(s32[2]{0:T(128)S(1)} %pad_add_fusion.pos, f32[2,8,1024]{2,1,0:T(8,128)S(1)} %get-tuple-element.24.own, f32[2,8,1024]{2,1,0:T(8,128)S(1)} %collective-permute-done.11.sib, f32[2,8,1024]{2,1,0:T(8,128)S(1)} %collective-permute-done.6.near_a, ...), custom_call_target="tpu_custom_call" | custom-call | tf_op jit(solution)/shard_map/powers/pallas_call | solution.py:355
  96.0 3.5 %collective-permute-start.13 = (f32[3,8,1024]{2,1,0:T(8,128)S(1)}, f32[3,8,1024]{2,1,0:T(8,128)S(1)}, u32[]{:S(2)}, u32[]{:S(2)}) collective-permute-start(f32[3,8,1024]{2,1,0:T(8,128)S(1)} %get-tuple-element.31), channel_id=1, source_target_pairs={{0,128},{64,192},{128,256},{192,320},{256,384},{320,448},{1,129},{... | collective-permute-start | bytes 294920 | tf_op jit(solution)/shard_map/ppermute | solution.py:375
  101.5 13.6 %collective-permute-start.18 = (f32[3,8,2048]{2,1,0:T(8,128)S(1)}, f32[3,8,2048]{2,1,0:T(8,128)S(1)}, u32[]{:S(2)}, u32[]{:S(2)}) collective-permute-start(f32[3,8,2048]{2,1,0:T(8,128)S(1)} %collective-permute-done.17), channel_id=1, source_target_pairs={{8,64},{73,65},{10,66},{75,67},{12,68},{77,69},{14,70},{79,71},{64... | collective-permute-start | bytes 589832 | tf_op jit(solution)/shard_map/ppermute | solution.py:472
  115.2 1.9 %collective-permute-start.16 = (f32[2,8,1024]{2,1,0:T(8,128)S(1)}, f32[2,8,1024]{2,1,0:T(8,128)S(1)}, u32[]{:S(2)}, u32[]{:S(2)}) collective-permute-start(f32[2,8,1024]{2,1,0:T(8,128)S(1)} %slice.4), channel_id=1, source_target_pairs={{0,64},{64,128},{128,192},{192,256},{256,320},{320,384},{384,448},... | collective-permute-start | bytes 196616 | tf_op jit(solution)/shard_map/ppermute | solution.py:375
  117.1 7.3 %collective-permute-done.18.detail = f32[3,8,2048]{2,1,0:T(8,128)S(1)} collective-permute-done((f32[3,8,2048]{2,1,0:T(8,128)S(1)}, f32[3,8,2048]{2,1,0:T(8,128)S(1)}, u32[]{:S(2)}, u32[]{:S(2)}) %collective-permute-start.18) | collective-permute-done | bytes 196640 | tf_op jit(solution)/shard_map/ppermute | solution.py:472
  124.4 8.9 %collective-permute-done.16.other = f32[2,8,1024]{2,1,0:T(8,128)S(1)} collective-permute-done((f32[2,8,1024]{2,1,0:T(8,128)S(1)}, f32[2,8,1024]{2,1,0:T(8,128)S(1)}, u32[]{:S(2)}, u32[]{:S(2)}) %collective-permute-start.16) | collective-permute-done | bytes 65568 | tf_op jit(solution)/shard_map/ppermute | solution.py:375
  (27 shorter events, 7.4 us)
Async XLA Ops:
  0.6 37.5 %copy-start = (f32[1,3,8,2048]{3,2,1,0:T(8,128)S(1)}, f32[1,3,8,2048]{3,2,1,0:T(8,128)}, u32[]{:S(2)}) copy-start(f32[1,3,8,2048]{3,2,1,0:T(8,128)} %param.2) | copy-start | bytes 589828
  0.6 37.5 %copy-start.1 = (f32[8,2048]{1,0:T(8,128)S(1)}, f32[8,2048]{1,0:T(8,128)}, u32[]{:S(2)}) copy-start(f32[8,2048]{1,0:T(8,128)} %field.3) | copy-start | bytes 196612
  1.7 23.0 %collective-permute-start.2 = (f32[4,8,2048]{2,1,0:T(8,128)S(1)}, f32[4,8,2048]{2,1,0:T(8,128)S(1)}, u32[]{:S(2)}, u32[]{:S(2)}) collective-permute-start(f32[4,8,2048]{2,1,0:T(8,128)S(1)} %pad_maximum_fusion), channel_id=1, source_target_pairs={{1,4},{3,6},{4,1},{5,8},{6,3},{7,10},{8,5},{9,12},{10,7},{11,14},{... | collective-permute-start | bytes 786440 | tf_op jit(solution)/shard_map/ppermute | solution.py:370
  12.9 11.7 %collective-permute-start.1 = (f32[4,8,2048]{2,1,0:T(8,128)S(1)}, f32[4,8,2048]{2,1,0:T(8,128)S(1)}, u32[]{:S(2)}, u32[]{:S(2)}) collective-permute-start(f32[4,8,2048]{2,1,0:T(8,128)S(1)} %pad_maximum_fusion), channel_id=1, source_target_pairs={{0,2},{1,3},{2,0},{3,1},{4,6},{5,7},{6,4},{7,5},{8,10},{9,11},{10,... | collective-permute-start | bytes 786440 | tf_op jit(solution)/shard_map/ppermute | solution.py:370
  16.7 15.9 %collective-permute-start = (f32[4,8,2048]{2,1,0:T(8,128)S(1)}, f32[4,8,2048]{2,1,0:T(8,128)S(1)}, u32[]{:S(2)}, u32[]{:S(2)}) collective-permute-start(f32[4,8,2048]{2,1,0:T(8,128)S(1)} %pad_maximum_fusion), channel_id=1, source_target_pairs={{2,4},{3,5},{4,2},{5,3},{6,8},{7,9},{8,6},{9,7},{10,12},{11,13},{1... | collective-permute-start | bytes 786440 | tf_op jit(solution)/shard_map/ppermute | solution.py:370
  18.8 18.3 %collective-permute-start.3 = (f32[4,8,2048]{2,1,0:T(8,128)S(1)}, f32[4,8,2048]{2,1,0:T(8,128)S(1)}, u32[]{:S(2)}, u32[]{:S(2)}) collective-permute-start(f32[4,8,2048]{2,1,0:T(8,128)S(1)} %pad_maximum_fusion), channel_id=1, source_target_pairs={{0,1},{1,0},{2,3},{3,2},{4,5},{5,4},{6,7},{7,6},{8,9},{9,8},{10,11... | collective-permute-start | bytes 786440 | tf_op jit(solution)/shard_map/ppermute | solution.py:370
  32.7 4.4 %collective-permute-start.4 = (f32[4,8,2048]{2,1,0:T(8,128)S(1)}, f32[4,8,2048]{2,1,0:T(8,128)S(1)}, u32[]{:S(2)}, u32[]{:S(2)}) collective-permute-start(f32[4,8,2048]{2,1,0:T(8,128)S(1)} %collective-permute-done.near_a), channel_id=1, source_target_pairs={{0,1},{1,0},{2,3},{3,2},{4,5},{5,4},{6,7},{7,6},{8,9},{9,8},{10,11... | collective-permute-start | bytes 786440 | tf_op jit(solution)/shard_map/ppermute | solution.py:370
  34.6 3.6 %collective-permute-start.5 = (f32[4,8,2048]{2,1,0:T(8,128)S(1)}, f32[4,8,2048]{2,1,0:T(8,128)S(1)}, u32[]{:S(2)}, u32[]{:S(2)}) collective-permute-start(f32[4,8,2048]{2,1,0:T(8,128)S(1)} %collective-permute-done.1.near_b), channel_id=1, source_target_pairs={{0,1},{1,0},{2,3},{3,2},{4,5},{5,4},{6,7},{7,6},{8,9},{9,8},{10,11... | collective-permute-start | bytes 786440 | tf_op jit(solution)/shard_map/ppermute | solution.py:370
  52.5 17.6 %collective-permute-start.11 = (f32[2,8,1024]{2,1,0:T(8,128)S(1)}, f32[2,8,1024]{2,1,0:T(8,128)S(1)}, u32[]{:S(2)}, u32[]{:S(2)}) collective-permute-start(f32[2,8,1024]{2,1,0:T(8,128)S(1)} %get-tuple-element.24.own), channel_id=1, source_target_pairs={{0,1},{1,0},{2,3},{3,2},{4,5},{5,4},{6,7},{7,6},{8,9},{9,8},{10,11... | collective-permute-start | bytes 196616 | tf_op jit(solution)/shard_map/ppermute | solution.py:370
  54.8 25.0 %collective-permute-start.10 = (f32[2,8,1024]{2,1,0:T(8,128)S(1)}, f32[2,8,1024]{2,1,0:T(8,128)S(1)}, u32[]{:S(2)}, u32[]{:S(2)}) collective-permute-start(f32[2,8,1024]{2,1,0:T(8,128)S(1)} %get-tuple-element.24.own), channel_id=1, source_target_pairs={{1,6},{3,8},{5,10},{6,1},{7,12},{8,3},{9,14},{10,5},{11,16},{12,7}... | collective-permute-start | bytes 196616 | tf_op jit(solution)/shard_map/ppermute | solution.py:370
  61.1 18.7 %collective-permute-start.9 = (f32[2,8,1024]{2,1,0:T(8,128)S(1)}, f32[2,8,1024]{2,1,0:T(8,128)S(1)}, u32[]{:S(2)}, u32[]{:S(2)}) collective-permute-start(f32[2,8,1024]{2,1,0:T(8,128)S(1)} %get-tuple-element.24.own), channel_id=1, source_target_pairs={{0,4},{1,5},{2,6},{3,7},{4,0},{5,1},{6,2},{7,3},{8,12},{9,13},{10,... | collective-permute-start | bytes 196616 | tf_op jit(solution)/shard_map/ppermute | solution.py:370
  63.9 15.9 %collective-permute-start.8 = (f32[2,8,1024]{2,1,0:T(8,128)S(1)}, f32[2,8,1024]{2,1,0:T(8,128)S(1)}, u32[]{:S(2)}, u32[]{:S(2)}) collective-permute-start(f32[2,8,1024]{2,1,0:T(8,128)S(1)} %get-tuple-element.24.own), channel_id=1, source_target_pairs={{4,8},{5,9},{6,10},{7,11},{8,4},{9,5},{10,6},{11,7},{12,16},{13,17... | collective-permute-start | bytes 196616 | tf_op jit(solution)/shard_map/ppermute | solution.py:370
  67.4 12.4 %collective-permute-start.7 = (f32[2,8,1024]{2,1,0:T(8,128)S(1)}, f32[2,8,1024]{2,1,0:T(8,128)S(1)}, u32[]{:S(2)}, u32[]{:S(2)}) collective-permute-start(f32[2,8,1024]{2,1,0:T(8,128)S(1)} %get-tuple-element.24.own), channel_id=1, source_target_pairs={{0,2},{1,3},{2,0},{3,1},{4,6},{5,7},{6,4},{7,5},{8,10},{9,11},{10,... | collective-permute-start | bytes 196616 | tf_op jit(solution)/shard_map/ppermute | solution.py:370
  70.1 13.7 %collective-permute-start.6 = (f32[2,8,1024]{2,1,0:T(8,128)S(1)}, f32[2,8,1024]{2,1,0:T(8,128)S(1)}, u32[]{:S(2)}, u32[]{:S(2)}) collective-permute-start(f32[2,8,1024]{2,1,0:T(8,128)S(1)} %get-tuple-element.24.own), channel_id=1, source_target_pairs={{2,4},{3,5},{4,2},{5,3},{6,8},{7,9},{8,6},{9,7},{10,12},{11,13},{1... | collective-permute-start | bytes 196616 | tf_op jit(solution)/shard_map/ppermute | solution.py:370
  83.8 5.1 %collective-permute-start.12 = (f32[8,8,1024]{2,1,0:T(8,128)S(1)}, f32[8,8,1024]{2,1,0:T(8,128)S(1)}, u32[]{:S(2)}, u32[]{:S(2)}) collective-permute-start(f32[8,8,1024]{2,1,0:T(8,128)S(1)} %pad_maximum_fusion.1), channel_id=1, source_target_pairs={{0,1},{1,0},{2,3},{3,2},{4,5},{5,4},{6,7},{7,6},{8,9},{9,8},{10,11... | collective-permute-start | bytes 786440 | tf_op jit(solution)/shard_map/ppermute | solution.py:370
  87.0 14.5 %collective-permute-start.17 = (f32[3,8,2048]{2,1,0:T(8,128)S(1)}, f32[3,8,2048]{2,1,0:T(8,128)S(1)}, u32[]{:S(2)}, u32[]{:S(2)}) collective-permute-start(f32[3,8,2048]{2,1,0:T(8,128)S(1)} %get-tuple-element.34), channel_id=1, source_target_pairs={{0,8},{1,73},{2,10},{3,75},{4,12},{5,77},{6,14},{7,79},{8,64},{9,1... | collective-permute-start | bytes 589832 | tf_op jit(solution)/shard_map/ppermute | solution.py:455
  96.0 19.1 %collective-permute-start.13 = (f32[3,8,1024]{2,1,0:T(8,128)S(1)}, f32[3,8,1024]{2,1,0:T(8,128)S(1)}, u32[]{:S(2)}, u32[]{:S(2)}) collective-permute-start(f32[3,8,1024]{2,1,0:T(8,128)S(1)} %get-tuple-element.31), channel_id=1, source_target_pairs={{0,128},{64,192},{128,256},{192,320},{256,384},{320,448},{1,129},{... | collective-permute-start | bytes 294920 | tf_op jit(solution)/shard_map/ppermute | solution.py:375
  99.5 15.6 %collective-permute-start.14 = (f32[3,8,1024]{2,1,0:T(8,128)S(1)}, f32[3,8,1024]{2,1,0:T(8,128)S(1)}, u32[]{:S(2)}, u32[]{:S(2)}) collective-permute-start(f32[3,8,1024]{2,1,0:T(8,128)S(1)} %get-tuple-element.32), channel_id=1, source_target_pairs={{0,256},{64,320},{128,384},{192,448},{1,257},{65,321},{129,385},{1... | collective-permute-start | bytes 294920 | tf_op jit(solution)/shard_map/ppermute | solution.py:375
  100.8 14.3 %collective-permute-start.15 = (f32[3,8,1024]{2,1,0:T(8,128)S(1)}, f32[3,8,1024]{2,1,0:T(8,128)S(1)}, u32[]{:S(2)}, u32[]{:S(2)}) collective-permute-start(f32[3,8,1024]{2,1,0:T(8,128)S(1)} %get-tuple-element.33), channel_id=1, source_target_pairs={{0,384},{64,448},{1,385},{65,449},{2,386},{66,450},{3,387},{67,451... | collective-permute-start | bytes 294920 | tf_op jit(solution)/shard_map/ppermute | solution.py:375
  101.5 22.9 %collective-permute-start.18 = (f32[3,8,2048]{2,1,0:T(8,128)S(1)}, f32[3,8,2048]{2,1,0:T(8,128)S(1)}, u32[]{:S(2)}, u32[]{:S(2)}) collective-permute-start(f32[3,8,2048]{2,1,0:T(8,128)S(1)} %collective-permute-done.17), channel_id=1, source_target_pairs={{8,64},{73,65},{10,66},{75,67},{12,68},{77,69},{14,70},{79,71},{64... | collective-permute-start | bytes 589832 | tf_op jit(solution)/shard_map/ppermute | solution.py:472
  115.2 18.1 %collective-permute-start.16 = (f32[2,8,1024]{2,1,0:T(8,128)S(1)}, f32[2,8,1024]{2,1,0:T(8,128)S(1)}, u32[]{:S(2)}, u32[]{:S(2)}) collective-permute-start(f32[2,8,1024]{2,1,0:T(8,128)S(1)} %slice.4), channel_id=1, source_target_pairs={{0,64},{64,128},{128,192},{192,256},{256,320},{320,384},{384,448},... | collective-permute-start | bytes 196616 | tf_op jit(solution)/shard_map/ppermute | solution.py:375
